TPU v7x, 32 devices: a whole 2x2x4 slice. The times are simulated.
32 devices in a mesh: fsdp: 4 (over z), seq: 8 (over y, x, core).
Axes of the slice: x: 2, y: 2, z: 4, core: 2. Of those that a mesh axis runs over, the one named last changes fastest.
Arguments:
- tokens: bfloat16 [1792, 4096], P(('fsdp', 'seq')), may hold values from -6 to 6
- grad_out: bfloat16 [1792, 4096], P(('fsdp', 'seq')), may hold values from -6 to 6
- gate_weight: bfloat16 [4096, 14336], P('fsdp', 'seq'), may hold values from -0.09375 to 0.09375
- up_weight: bfloat16 [4096, 14336], P('fsdp', 'seq'), may hold values from -0.09375 to 0.09375
- down_weight: bfloat16 [14336, 4096], P('seq', 'fsdp'), may hold values from -0.09375 to 0.09375
- keep_mask: int32 [8, 112], P(None, 'seq'), may hold values from 0 to 1, as said below
- task_ids: int32 [1792], P('fsdp'), may hold values from 0 to 7
Outputs:
- layer_out: bfloat16 [1792, 4096], P(('fsdp', 'seq'))
- input_grad: bfloat16 [1792, 4096], P(('fsdp', 'seq'))
Inputs may be any that keep to these rules, and one draw needn't show every extreme that they name: `keep_mask`: entries are 0 or 1. In each aligned group of 14 consecutive blocks at most 8 blocks are kept by some task, and exactly 8 in at least one group; the other blocks of a group are kept by no task.
All inputs are finite; a program needn't handle non-finite values.
Results may differ from a plain program's by a relative error of at most 0.014.
Values may be sent and summed in bfloat16 or wider, within the bound.
No kernel may reach another device: no remote copies, remote signals or barrier semaphores. Data moves between devices by JAX's collectives and lax.ppermute only.
A program may use at most 128 MiB of HBM per device.

v0:
```python
import jax
import jax.numpy as jnp
from jax import lax
from jax.sharding import PartitionSpec as P


def pick_columns(weight, chosen, block_count, block_width):
    model_width = weight.shape[0]
    shaped = weight.reshape(model_width, block_count, block_width)
    return jnp.take(shaped, chosen, axis=1).reshape(model_width, chosen.shape[0] * block_width)


def pick_rows(weight, chosen, block_count, block_width):
    columns = weight.shape[1]
    shaped = weight.reshape(block_count, block_width, columns)
    return jnp.take(shaped, chosen, axis=0).reshape(chosen.shape[0] * block_width, columns)


def transposed(left, right):
    return lax.dot_general(
        left, right, (((1,), (1,)), ((), ())), preferred_element_type=jnp.float32
    )


def local(tokens, grad_out, gate_weight, up_weight, down_weight, keep_mask, task_ids):
    token_rows, grad_rows = (
        lax.all_gather(tokens, "seq", axis=0, tiled=True),
        lax.all_gather(grad_out, "seq", axis=0, tiled=True),
    )
    task_count, block_count = keep_mask.shape
    local_width = gate_weight.shape[1]
    block_width = local_width // block_count
    kept_count = block_count * 4 // 7
    alive_blocks = jnp.max(keep_mask, axis=0)
    ranking = jnp.argsort(
        (1 - alive_blocks) * block_count + jnp.arange(block_count, dtype=jnp.int32)
    )
    chosen = ranking[:kept_count]
    keep_local = jnp.take(keep_mask, chosen, axis=1)
    gate_pick = pick_columns(gate_weight, chosen, block_count, block_width)
    up_pick = pick_columns(up_weight, chosen, block_count, block_width)
    down_pick = pick_rows(down_weight, chosen, block_count, block_width)
    gate_full, up_full = (
        lax.all_gather(gate_pick, "fsdp", axis=0, tiled=True),
        lax.all_gather(up_pick, "fsdp", axis=0, tiled=True),
    )
    down_full = lax.all_gather(down_pick, "fsdp", axis=1, tiled=True)
    onehot_tasks = (task_ids[:, None] == jnp.arange(task_count, dtype=jnp.int32)[None, :]).astype(
        jnp.float32
    )
    row_keep = jnp.dot(onehot_tasks, keep_local.astype(jnp.float32))
    neuron_mask = jnp.repeat(row_keep, block_width, axis=1)
    gate_pre = jnp.dot(token_rows, gate_full, preferred_element_type=jnp.float32)
    up_pre = jnp.dot(token_rows, up_full, preferred_element_type=jnp.float32)
    logistic = jax.nn.sigmoid(gate_pre)
    activated = gate_pre * logistic
    hidden = (activated * up_pre * neuron_mask).astype(jnp.bfloat16)
    layer_out = lax.psum_scatter(
        jnp.dot(hidden, down_full, preferred_element_type=jnp.float32).astype(jnp.bfloat16),
        "seq",
        scatter_dimension=0,
        tiled=True,
    )
    hidden_grad = transposed(grad_rows, down_full)
    masked_grad = hidden_grad * neuron_mask
    gate_grad = (masked_grad * up_pre * logistic * (1.0 + gate_pre * (1.0 - logistic))).astype(
        jnp.bfloat16
    )
    up_grad = (masked_grad * activated).astype(jnp.bfloat16)
    input_grad = lax.psum_scatter(
        (transposed(gate_grad, gate_full) + transposed(up_grad, up_full)).astype(jnp.bfloat16),
        "seq",
        scatter_dimension=0,
        tiled=True,
    )
    return (layer_out, input_grad)


def solution(mesh):
    placed = (
        P(("fsdp", "seq"), None),
        P(("fsdp", "seq"), None),
        P("fsdp", "seq"),
        P("fsdp", "seq"),
        P("seq", "fsdp"),
        P(None, "seq"),
        P("fsdp"),
    )
    return jax.shard_map(
        local,
        mesh=mesh,
        in_specs=placed,
        out_specs=(P(("fsdp", "seq"), None), P(("fsdp", "seq"), None)),
        check_vma=False,
    )
```

profile of v0, /device:TPU:0, one launch (start us, length us, event | category | flops | bytes accessed | tf_op | source)
XLA Modules:
  0.0 668.8 jit_solution(7754367115990336582)
XLA Ops:
  7.9 5.9 copy.17
  13.9 5.9 copy.18
  19.8 6.0 copy.20
  25.8 5.9 copy.21
  31.7 1.2 sort.17
  33.0 4.7 gather_fusion.2
  37.7 4.2 gather_fusion.3
  41.9 4.1 select_bitcast_fusion.1
  45.9 4.0 copy.19
  50.0 2.7 copy.22
  53.3 2.7 gather_fusion.1
  56.1 1.7 bitcast_select_fusion
  59.0 143.0 %all-gather.6.cloned.1.call-done = bf16[4096,1024]{0,1:T(8,128)(2,1)} async-done(((bf16[1024,1024]{0,1:T(8,128)(2,1)}), bf16[4096,1024]{0,1:T(8,128)(2,1)}) %all-gather.6.cloned.1.call-update) | async-done | bytes 8388624 | tf_op jit(solution)/shard_map/all_gather | solution.py:44
  201.9 9.6 %fusion.22 = f32[1024,448]{0,1:T(8,128)} fusion(bf16[4096,1024]{0,1:T(8,128)(2,1)} %all-gather.6.cloned.1.call-done, bf16[448,4096]{1,0:T(8,128)(2,1)} %all-gather.8.cloned.1.call-done), kind=kOutput, calls=%fused_computation.43 | convolution fusion | flops 3758096384 | bytes 13893632 | tf_op jit(solution)/shard_map/dot_general | solution.py:53
  211.6 139.8 %all-gather.10.cloned.1.call-done = bf16[4096,1024]{0,1:T(8,128)(2,1)} async-done(((bf16[1024,1024]{0,1:T(8,128)(2,1)}), bf16[4096,1024]{0,1:T(8,128)(2,1)}) %all-gather.10.cloned.1.call-update) | async-done | bytes 8388624 | tf_op jit(solution)/shard_map/all_gather | solution.py:45
  351.4 9.7 %fusion.23 = f32[1024,448]{0,1:T(8,128)} fusion(bf16[4096,1024]{0,1:T(8,128)(2,1)} %all-gather.10.cloned.1.call-done, bf16[448,4096]{1,0:T(8,128)(2,1)} %all-gather.8.cloned.1.call-done), kind=kOutput, calls=%fused_computation.44 | convolution fusion | flops 3758096384 | bytes 13893632 | tf_op jit(solution)/shard_map/dot_general | solution.py:54
  361.0 24.8 %all-gather.14.cloned.1.call-done = bf16[448,4096]{1,0:T(8,128)(2,1)} async-done(((bf16[56,4096]{1,0:T(8,128)(2,1)}), bf16[448,4096]{1,0:T(8,128)(2,1)}) %all-gather.14.cloned.1.call-update) | async-done | bytes 3670032 | tf_op jit(solution)/shard_map/all_gather | solution.py:28
  385.8 151.1 %all-gather.12.cloned.1.call-done = bf16[1024,4096]{1,0:T(8,128)(2,1)} async-done(((bf16[1024,1024]{1,0:T(8,128)(2,1)}), bf16[1024,4096]{1,0:T(8,128)(2,1)}) %all-gather.12.cloned.1.call-update) | async-done | bytes 8388624 | tf_op jit(solution)/shard_map/all_gather | solution.py:47
  537.5 10.0 %bitcast_multiply_fusion = f32[448,1024]{1,0:T(8,128)} fusion(f32[56,8,8,128]{3,2,1,0:T(8,128)S(1)} %bitcast.73, bf16[1024,4096]{1,0:T(8,128)(2,1)} %all-gather.12.cloned.1.call-done, bf16[448,4096]{1,0:T(8,128)(2,1)} %all-gather.14.cloned.1.call-done), kind=kOutput, calls=%fused_computation.9 | convolution fusion | flops 3758555136 | bytes 15728640 | tf_op jit(solution)/shard_map/dot_general | solution.py:20
  547.5 7.0 %fusion.8 = f32[448,4096]{1,0:T(8,128)S(1)} fusion(bf16[4096,1024]{0,1:T(8,128)(2,1)S(1)} %bitcast.77, f32[448,1024]{1,0:T(8,128)} %bitcast_multiply_fusion, f32[1024,448]{0,1:T(8,128)} %fusion.23, f32[1024,448]{0,1:T(8,128)S(1)} %copy-done.2), kind=kOutput, calls=%fused_computation.25 | convolution fusion | flops 3762683904 | bytes 21233664 | tf_op jit(solution)/shard_map/dot_general | solution.py:20
  554.6 7.2 %add_convert_fusion = bf16[448,4096]{1,0:T(8,128)(2,1)} fusion(f32[448,4096]{1,0:T(8,128)S(1)} %fusion.8, bf16[4096,1024]{0,1:T(8,128)(2,1)S(1)} %bitcast.79, f32[448,1024]{1,0:T(8,128)} %bitcast_multiply_fusion, f32[1024,448]{0,1:T(8,128)S(1)} %copy-done.2), kind=kOutput, calls=%fused_computation.4 | convolution fusion | flops 3764518912 | bytes 23068672 | tf_op jit(solution)/shard_map/dot_general | solution.py:20
  561.8 10.8 %convolution_convert_fusion = bf16[448,4096]{1,0:T(8,128)(2,1)} fusion(bf16[1024,4096]{1,0:T(8,128)(2,1)} %all-gather.12.cloned.1.call-done, f32[1024,448]{0,1:T(8,128)} %fusion.23, f32[56,8,8,128]{3,2,1,0:T(8,128)S(1)} %bitcast.74, f32[1024,448]{0,1:T(8,128)} %fusion.22), kind=kOutput, calls=%fused_computation.5 | convolution fusion | flops 3763142656 | bytes 17563648 | tf_op jit(solution)/shard_map/dot_general | solution.py:59
  572.7 36.2 %reduce-scatter.5.cloned.1.call-done = bf16[56,4096]{1,0:T(8,128)(2,1)} async-done(((bf16[448,4096]{1,0:T(8,128)(2,1)}), bf16[56,4096]{1,0:T(8,128)(2,1)}) %reduce-scatter.5.cloned.1.call-update) | async-done | bytes 458768 | tf_op jit(solution)/shard_map/reduce_scatter | solution.py:70
  608.8 53.2 %reduce-scatter.3.cloned.1.call-done = bf16[56,4096]{1,0:T(8,128)(2,1)} async-done(((bf16[448,4096]{1,0:T(8,128)(2,1)}), bf16[56,4096]{1,0:T(8,128)(2,1)}) %reduce-scatter.3.cloned.1.call-update) | async-done | bytes 458768 | tf_op jit(solution)/shard_map/reduce_scatter | solution.py:58
  (41 shorter events, 3.3 us)
Async XLA Ops:
  7.2 51.8 %all-gather.8.cloned.1.call-start = ((), (), s32[]{:S(2)}) async-start(), calls=%async_computation.3 | async-start | bytes 4128768 | tf_op jit(solution)/shard_map/all_gather | solution.py:27
  7.9 194.0 %all-gather.6.cloned.1.call-start = ((), (), s32[]{:S(2)}) async-start(), calls=%async_computation.2 | async-start | bytes 10485760 | tf_op jit(solution)/shard_map/all_gather | solution.py:44
  25.8 5.9 copy-start
  49.9 301.4 %all-gather.10.cloned.1.call-start = ((), (), s32[]{:S(2)}) async-start(), calls=%async_computation.4 | async-start | bytes 10485760 | tf_op jit(solution)/shard_map/all_gather | solution.py:45
  52.7 333.2 %all-gather.14.cloned.1.call-start = ((), (), s32[]{:S(2)}) async-start(), calls=%async_computation.7 | async-start | bytes 4128768 | tf_op jit(solution)/shard_map/all_gather | solution.py:28
  53.3 483.7 %all-gather.12.cloned.1.call-start = ((), (), s32[]{:S(2)}) async-start(), calls=%async_computation.5 | async-start | bytes 10485760 | tf_op jit(solution)/shard_map/all_gather | solution.py:47
  57.8 0.9 copy-start.1
  57.8 551.0 %reduce-scatter.5.cloned.1.call-start = ((), (), s32[]{:S(2)}) async-start(), calls=%async_computation.8 | async-start | bytes 4128768 | tf_op jit(solution)/shard_map/reduce_scatter | solution.py:70
  536.9 10.6 %slice-start = ((s8[8388608]{0:T(1024)(128)(4,1)}), s8[4194304]{0:T(1024)(128)(4,1)S(1)}, s32[]{:S(2)}) async-start(s8[8388608]{0:T(1024)(128)(4,1)} %bitcast.76), calls=%async_computation.9 | async-start | bytes 8388608
  537.5 10.1 %slice-start.1 = ((s8[8388608]{0:T(1024)(128)(4,1)}), s8[4194304]{0:T(1024)(128)(4,1)S(1)}, s32[]{:S(2)}) async-start(s8[8388608]{0:T(1024)(128)(4,1)} %bitcast.76), calls=%async_computation.10 | async-start | bytes 8388608
  537.5 10.0 %copy-start.2 = (f32[1024,448]{0,1:T(8,128)S(1)}, f32[1024,448]{0,1:T(8,128)}, u32[]{:S(2)}) copy-start(f32[1024,448]{0,1:T(8,128)} %fusion.22) | copy-start | bytes 5505028
  537.5 17.1 %slice-start.2 = ((s8[8388608]{0:T(1024)(128)(4,1)}), s8[4194304]{0:T(1024)(128)(4,1)S(1)}, s32[]{:S(2)}) async-start(s8[8388608]{0:T(1024)(128)(4,1)} %bitcast.78), calls=%async_computation.11 | async-start | bytes 8388608
  547.5 7.0 %slice-start.3 = ((s8[8388608]{0:T(1024)(128)(4,1)}), s8[4194304]{0:T(1024)(128)(4,1)S(1)}, s32[]{:S(2)}) async-start(s8[8388608]{0:T(1024)(128)(4,1)} %bitcast.78), calls=%async_computation.12 | async-start | bytes 8388608
  561.8 100.2 %reduce-scatter.3.cloned.1.call-start = ((), (), s32[]{:S(2)}) async-start(), calls=%async_computation.6 | async-start | bytes 4128768 | tf_op jit(solution)/shard_map/reduce_scatter | solution.py:58
Sparse Core Ops, SparseCore 0:
  9.9 37.6 all-gather.7
  50.0 151.8 all-gather.5
  203.5 147.8 all-gather.9
  353.1 32.6 all-gather.13
  387.3 149.6 all-gather.11
  561.9 46.8 reduce-scatter.4
  613.3 48.6 reduce-scatter.2
where the time goes:
time: 670 us; the launch traced here: 669 us
  waiting for transfers between devices  549 us (82%)
  matrix products  54.6 us (8%)
  local copies, waits for them, and re-layouts  43.3 us (6%)
  between operations  14.2 us (2%)
  other arithmetic  7.03 us (1%)
    all_gather x1, waiting for transfers between devices, local(): down_full = lax.all_gather(down_pick, 'fsdp', axis=1, tiled=True)  151 us
    all_gather x1, waiting for transfers between devices, local(): lax.all_gather(gate_pick, 'fsdp', axis=0, tiled=True)  143 us
    all_gather x1, waiting for transfers between devices, local(): lax.all_gather(up_pick, 'fsdp', axis=0, tiled=True)  140 us
    reduce_scatter x1, waiting for transfers between devices, local(): lax.psum_scatter(jnp.dot(hidden, down_full, preferred_element_type=jnp.fl...  53.2 us
    reduce_scatter x1, waiting for transfers between devices, local(): lax.psum_scatter((transposed(gate_grad, gate_full) + transposed(up_grad,...  36.2 us
    all_gather x1, waiting for transfers between devices, local(): lax.all_gather(grad_out, 'seq', axis=0, tiled=True)  24.8 us
    dot_general x3, matrix products, transposed(): lax.dot_general(left, right, (((1,), (1,)), ((), ())), preferred_element_...  24.2 us
  transfers between devices with their start and end apart: 7, of which 6 were waited for; matrix products, arithmetic and copies ran while one was open for 12% of the time, Pallas kernels for 0%

commit v1 on v0

v1 whole, which is shorter than its diff:
```python
import functools

import jax
import jax.numpy as jnp
from jax import lax
from jax.experimental import pallas as pl
from jax.experimental.pallas import tpu as pltpu
from jax.sharding import PartitionSpec as P

BF16, F32 = jnp.bfloat16, jnp.float32


def dot_t(left, right):
    return lax.dot_general(left, right, (((1,), (1,)), ((), ())), preferred_element_type=F32)


def dot(left, right):
    return jnp.dot(left, right, preferred_element_type=F32)


def pick_kernel(nf, kept, width, layer_ref, keep_ref, gate, up, down, *rest):
    sends, (down_out, keep_out) = rest[:nf], rest[nf : nf + 2]
    chosen, stage, down_stage, in_sems, out_sems = rest[nf + 2 :]
    tasks, blocks = keep_ref.shape
    for slot in range(kept):
        chosen[slot] = 0
    live = jnp.int32(0)
    flags = []
    for b in range(blocks):
        alive = keep_ref[0, b]
        for t in range(1, tasks):
            alive = jnp.maximum(alive, keep_ref[t, b])
        flags.append(alive)

        @pl.when((alive > 0) & (live < kept))
        def _(live=live, b=b):
            chosen[live] = b

        live = live + alive
    for b in range(blocks):

        @pl.when((flags[b] == 0) & (live < kept))
        def _(live=live, b=b):
            chosen[live] = b

        live = live + (1 - flags[b])
    layer = layer_ref[0]
    per = kept // nf
    arrivals = []

    def fetch(source, target):
        copy = pltpu.make_async_copy(source, target, in_sems.at[len(arrivals)])
        arrivals.append(copy)
        copy.start()

    order = [(p + 1) % nf for p in range(nf)]
    for p in order:
        dest = lax.bitwise_xor(layer, p)
        for i in range(per):
            block = pl.ds(pl.multiple_of(chosen[dest * per + i] * width, width), width)
            for half, source in enumerate((gate, up)):
                fetch(source.at[:, block], stage.at[p, :, pl.ds((half * per + i) * width, width)])
    for slot in range(kept):
        block = pl.ds(pl.multiple_of(chosen[slot] * width, width), width)
        fetch(down.at[block, :], down_stage.at[pl.ds(slot * width, width), :])
    for slot in range(kept):
        for t in range(tasks):
            keep_out[t, slot] = keep_ref[t, chosen[slot]]
    leaving = []
    for place, p in enumerate(order):
        for copy in arrivals[place * 2 * per : (place + 1) * 2 * per]:
            copy.wait()
        leaving.append(pltpu.make_async_copy(stage.at[p], sends[p], out_sems.at[p]))
        leaving[-1].start()
    for copy in arrivals[2 * kept :]:
        copy.wait()
    leaving.append(pltpu.make_async_copy(down_stage, down_out, out_sems.at[nf]))
    leaving[-1].start()
    for copy in leaving:
        copy.wait()


def pick(nf, f, keep_mask, gate_weight, up_weight, down_weight):
    tasks, blocks = keep_mask.shape
    deep, local_width = gate_weight.shape
    width = local_width // blocks
    kept = blocks * 4 // 7
    hidden = kept * width
    q = hidden // nf
    if kept % nf == 0:
        out = pl.pallas_call(
            functools.partial(pick_kernel, nf, kept, width),
            in_specs=[pl.BlockSpec(memory_space=pltpu.SMEM)] * 2 + [pl.BlockSpec(memory_space=pl.ANY)] * 3,
            out_specs=[pl.BlockSpec(memory_space=pl.ANY)] * (nf + 1) + [pl.BlockSpec(memory_space=pltpu.SMEM)],
            out_shape=[jax.ShapeDtypeStruct((deep, 2 * q), BF16)] * nf
            + [jax.ShapeDtypeStruct((hidden, down_weight.shape[1]), BF16), jax.ShapeDtypeStruct((tasks, kept), jnp.int32)],
            scratch_shapes=[
                pltpu.SMEM((kept,), jnp.int32),
                pltpu.VMEM((nf, deep, 2 * q), BF16),
                pltpu.VMEM((hidden, down_weight.shape[1]), BF16),
                pltpu.SemaphoreType.DMA((3 * kept,)),
                pltpu.SemaphoreType.DMA((nf + 1,)),
            ],
            compiler_params=pltpu.CompilerParams(vmem_limit_bytes=32 * 2**20),
        )(f.reshape(1), keep_mask, gate_weight, up_weight, down_weight)
        return out[:nf], out[nf], out[nf + 1]
    alive = jnp.max(keep_mask, axis=0)
    chosen = jnp.argsort((1 - alive) * blocks + jnp.arange(blocks, dtype=jnp.int32))[:kept]
    gate_pick, up_pick = (
        jnp.take(w.reshape(deep, blocks, width), chosen, axis=1).reshape(deep, hidden) for w in (gate_weight, up_weight)
    )
    down_pick = jnp.take(down_weight.reshape(blocks, width, -1), chosen, axis=0).reshape(hidden, -1)
    sends = [
        jnp.concatenate([lax.dynamic_slice_in_dim(w, (f ^ p) * q, q, 1) for w in (gate_pick, up_pick)], axis=1)
        for p in range(nf)
    ]
    return sends, down_pick, jnp.take(keep_mask, chosen, axis=1)


def from_layers(pieces, f):
    n = len(pieces)
    stacked = jnp.zeros((n, *pieces[0].shape), pieces[0].dtype)
    for p, piece in enumerate(pieces):
        if p:
            piece = lax.ppermute(piece, "fsdp", [(i, i ^ p) for i in range(n)])
        stacked = lax.dynamic_update_index_in_dim(stacked, piece, f ^ p, 0)
    return stacked


def line_scatter(unit, n, axis, me):
    up = down = None
    for k in range(1, n):
        ahead, behind = unit(jnp.clip(me + n - k, 0, n - 1)), unit(jnp.clip(me - n + k, 0, n - 1))
        if k > 1:
            ahead, behind = ahead + up.astype(F32), behind + down.astype(F32)
        up = lax.ppermute(ahead.astype(BF16), axis, [(i, i + 1) for i in range(k)])
        down = lax.ppermute(behind.astype(BF16), axis, [(i, i - 1) for i in range(n - k, n)])
    return unit(me) + up.astype(F32) + down.astype(F32)


def layer_scatter(rows_of, weight, n, chip, order):
    held = list(range(n))
    got = {d: [] for d in held}
    for bit in order:
        sent = [d for d in held if d >> bit & 1]
        held = [d for d in held if not d >> bit & 1]
        part = dot_t(jnp.concatenate([rows_of(chip ^ d) for d in sent]), weight)
        for piece in zip(*(got[d] for d in sent)):
            part = part + jnp.concatenate(piece).astype(F32)
        arrived = lax.ppermute(part.astype(BF16), "seq", [(i, i ^ (2 << bit)) for i in range(2 * n)])
        for d, piece in zip(sent, jnp.split(arrived, len(sent))):
            got[d ^ (1 << bit)].append(piece)
    total = dot_t(rows_of(chip), weight)
    for piece in got[0]:
        total = total + piece.astype(F32)
    return total


def local(nf, ns, tokens, grad_out, gate_weight, up_weight, down_weight, keep_mask, task_ids):
    f, s = lax.axis_index("fsdp"), lax.axis_index("seq")
    core, chip, chips = s & 1, s >> 1, ns // 2
    rows, wide = tokens.shape
    deep = wide // nf
    every = nf * ns * rows
    swap = [(i, i ^ 1) for i in range(ns)]

    with jax.named_scope("grad_rows"):
        ids = from_layers([task_ids.reshape(ns, rows)] * nf, f)
        grads = from_layers([lax.dynamic_slice_in_dim(grad_out, (f ^ p) * deep, deep, 1) for p in range(nf)], f)
    with jax.named_scope("pick"):
        sends, down_pick, keep_pick = pick(nf, f, keep_mask, gate_weight, up_weight, down_weight)
    hidden_width = down_pick.shape[0]
    q = hidden_width // nf

    with jax.named_scope("weights"):
        weight = from_layers(sends, f).reshape(wide, 2 * q)

    half = wide // 2
    with jax.named_scope("token_rows"):
        own_rows = lax.dynamic_slice_in_dim(tokens, core * half, half, 1)
        twin_rows = lax.ppermute(lax.dynamic_slice_in_dim(tokens, (1 - core) * half, half, 1), "seq", swap)
        token_rows = jnp.where(core == 0, jnp.stack([own_rows, twin_rows]), jnp.stack([twin_rows, own_rows]))
        token_rows = lax.all_gather(token_rows, "fsdp", axis=1, tiled=False)
        grads = lax.all_gather(grads.reshape(nf * rows, deep), "seq", axis=0, tiled=True)
        token_rows, grads = lax.optimization_barrier((token_rows, grads))
        same_core = [[i for i in range(ns) if i & 1 == c] for c in range(2)]
        token_rows = lax.all_gather(
            token_rows.reshape(2 * nf * rows, half), "seq", axis=0, tiled=True, axis_index_groups=same_core
        )

    with jax.named_scope("hidden_grad"):
        hidden_grad = line_scatter(
            lambda j: dot_t(grads, lax.dynamic_slice_in_dim(down_pick, j * q, q, 0)), nf, "fsdp", f
        )

    with jax.named_scope("twin_weights"):
        mine = lax.dynamic_slice_in_dim(weight, core * half, half, 0)
        other = lax.ppermute(lax.dynamic_slice_in_dim(weight, (1 - core) * half, half, 0), "seq", swap)
        both_weight = jnp.concatenate([mine, other], axis=1)

    with jax.named_scope("mask"):
        ids = ids.transpose(1, 0, 2).reshape(every)
        tasks, kept = keep_pick.shape
        onehot = (ids[:, None] == jnp.arange(tasks, dtype=jnp.int32)[None, :]).astype(BF16)
        keep_columns = jnp.repeat(keep_pick.astype(BF16), hidden_width // kept, axis=1)
        mask = dot(onehot, lax.dynamic_slice_in_dim(keep_columns, f * q, q, 1))

    with jax.named_scope("elementwise"):
        pre = dot(token_rows, both_weight)
        pre = pre[:, : 2 * q] + lax.ppermute(pre[:, 2 * q :].astype(BF16), "seq", swap).astype(F32)
        gate_pre, up_pre = pre[:, :q], pre[:, q:]
        logistic = jax.nn.sigmoid(gate_pre)
        activated = gate_pre * logistic
        hidden = (activated * up_pre * mask).astype(BF16)
        masked_grad = hidden_grad * mask
        gate_grad = (masked_grad * up_pre * logistic * (1.0 + gate_pre * (1.0 - logistic))).astype(BF16)
        up_grad = (masked_grad * activated).astype(BF16)

    with jax.named_scope("layer_out"):
        hidden_all = lax.all_gather(hidden, "fsdp", axis=1, tiled=True)
        out_part = dot(hidden_all, down_pick).astype(BF16)
        out = lax.psum_scatter(out_part, "seq", scatter_dimension=0, tiled=True)
        out = lax.all_to_all(out.reshape(nf, rows, deep), "fsdp", 0, 0, tiled=False)
        layer_out = out.transpose(1, 0, 2).reshape(rows, wide)

    with jax.named_scope("input_grad"):
        own = jnp.concatenate([gate_grad, up_grad], axis=1)
        both = jnp.concatenate([own, lax.ppermute(own, "seq", swap)], axis=1).reshape(chips, every // chips, 4 * q)
        rows_of = lambda c: lax.dynamic_index_in_dim(both, c, 0, keepdims=False)
        bits = list(range(chips.bit_length() - 1))
        first = layer_scatter(rows_of, both_weight[: half // 2], chips, chip, bits)
        second = layer_scatter(rows_of, both_weight[half // 2 :], chips, chip, bits[::-1])
        part = jnp.concatenate([first, second], axis=1).reshape(2, nf, rows, half)
        total = line_scatter(
            lambda j: lax.dynamic_index_in_dim(part, j, 1, keepdims=False), nf, "fsdp", f
        ).astype(BF16)
        here = lax.dynamic_index_in_dim(total, core, 0, keepdims=False)
        there = lax.ppermute(lax.dynamic_index_in_dim(total, 1 - core, 0, keepdims=False), "seq", swap)
        input_grad = jnp.where(
            core == 0, jnp.concatenate([here, there], axis=1), jnp.concatenate([there, here], axis=1)
        )
    return layer_out, input_grad


def solution(mesh):
    placed = (
        P(("fsdp", "seq"), None),
        P(("fsdp", "seq"), None),
        P("fsdp", "seq"),
        P("fsdp", "seq"),
        P("seq", "fsdp"),
        P(None, "seq"),
        P("fsdp"),
    )
    return jax.shard_map(
        functools.partial(local, mesh.shape["fsdp"], mesh.shape["seq"]),
        mesh=mesh,
        in_specs=placed,
        out_specs=(P(("fsdp", "seq"), None), P(("fsdp", "seq"), None)),
        check_vma=False,
    )
```

time: 670 us -> 465 us (0.69)
  waiting for transfers between devices: 549 us -> 265 us
  starting transfers between devices: 0.46 us -> 71 us
  local copies, waits for them, and re-layouts: 43.3 us -> 29.6 us
  matrix products: 54.6 us -> 63.1 us
  other arithmetic: 7.03 us -> 15.5 us
    all_gather x5 -> x4, waiting for transfers between devices: 459 us -> 65.6 us  [the longest x1 37.1 us: local(): lax.all_gather(grads.reshape(nf * rows, deep), 'seq', axis=0, tiled=True)]
    ppermute x0 -> x30, waiting for transfers between devices: none -> 187 us  [the longest x9 93.2 us: from_layers(): piece = lax.ppermute(piece, 'fsdp', [(i, i ^ p) for i in range(n)])]
    reduce_scatter x2 -> x1, waiting for transfers between devices: 89.3 us -> 0.02 us  [local(): out = lax.psum_scatter(out_part, 'seq', scatter_dimension=0, tiled=True)]
    ppermute x0 -> x30, starting transfers between devices: none -> 67.1 us  [the longest x6 39 us: line_scatter(): up = lax.ppermute(ahead.astype(BF16), axis, [(i, i + 1) for i in range(k)])]
    all_to_all x0 -> x1, waiting for transfers between devices: none -> 13.1 us  [local(): out = lax.all_to_all(out.reshape(nf, rows, deep), 'fsdp', 0, 0, tiled=False)]
    gather x4 -> x0, local copies, waits for them, and re-layouts: 12.2 us -> none  [the longest x2 8.89 us: pick_columns(): jnp.take(shaped, chosen, axis=1)]
    reshape x2, local copies, waits for them, and re-layouts: 11.8 us -> 0.88 us  [the longest x1 0.8 us: local(): layer_out = out.transpose(1, 0, 2).reshape(rows, wide)]
    dot_general x7 -> x16, matrix products: 54.6 us -> 63.1 us  [the longest x13 40.4 us: dot_t(): lax.dot_general(left, right, (((1,), (1,)), ((), ())), preferred_element_...]
  transfers between devices with their start and end apart: 7 -> 36, of which waited for: 6 -> 20; matrix products, arithmetic and copies ran while one was open for 12% -> 20% of each run, Pallas kernels for 0% -> 1%
where the time goes in v1:
time: 465 us; the launch traced here: 463 us
  waiting for transfers between devices  265 us (57%)
  starting transfers between devices  71 us (15%)
  matrix products  63.1 us (14%)
  local copies, waits for them, and re-layouts  29.6 us (6%)
  other arithmetic  15.5 us (3%)
  between operations  14.4 us (3%)
    ppermute x9, waiting for transfers between devices, from_layers(): piece = lax.ppermute(piece, 'fsdp', [(i, i ^ p) for i in range(n)])  93.2 us
    dot_general x13, matrix products, dot_t(): lax.dot_general(left, right, (((1,), (1,)), ((), ())), preferred_element_...  40.4 us
    ppermute x4, waiting for transfers between devices, layer_scatter(): lax.ppermute(part.astype(BF16), 'seq', [(i, i ^ 2 << bit) for i in range(...  40.1 us
    ppermute x6, starting transfers between devices, line_scatter(): up = lax.ppermute(ahead.astype(BF16), axis, [(i, i + 1) for i in range(k)])  39 us
    all_gather x1, waiting for transfers between devices, local(): lax.all_gather(grads.reshape(nf * rows, deep), 'seq', axis=0, tiled=True)  37.1 us
    ppermute x6, waiting for transfers between devices, line_scatter(): up = lax.ppermute(ahead.astype(BF16), axis, [(i, i + 1) for i in range(k)])  32.8 us
    all_gather x1, waiting for transfers between devices, local(): token_rows = lax.all_gather(token_rows, 'fsdp', axis=1, tiled=False)  28.5 us
    dot_general x3, matrix products, dot(): return jnp.dot(left, right, preferred_element_type=F32)  22.7 us
  transfers between devices with their start and end apart: 36, of which 20 were waited for; matrix products, arithmetic and copies ran while one was open for 20% of the time, Pallas kernels for 1%

profile of v1, /device:TPU:0, one launch (start us, length us, event | category | flops | bytes accessed | tf_op | source)
XLA Modules:
  0.0 463.3 jit_solution(459807510138807647)
XLA Ops:
  17.5 10.2 %collective-permute-done.2 = bf16[56,1024]{1,0:T(8,128)(2,1)S(1)} collective-permute-done((bf16[56,1024]{1,0:T(8,128)(2,1)S(1)}, bf16[56,1024]{1,0:T(8,128)(2,1)S(1)}, u32[]{:S(2)}, u32[]{:S(2)}) %collective-permute-start.2) | collective-permute-done | bytes 114720 | tf_op jit(solution)/shard_map/grad_rows/ppermute | solution.py:125
  28.6 28.5 %all-gather.5.cloned.1.call-done = bf16[2,4,56,2048]{3,2,1,0:T(8,128)(2,1)} async-done(((bf16[2,1,56,2048]{3,2,1,0:T(8,128)(2,1)}), bf16[2,4,56,2048]{3,2,1,0:T(8,128)(2,1)}) %all-gather.5.cloned.1.call-update) | async-done | bytes 1835024 | tf_op jit(solution)/shard_map/token_rows/all_gather | solution.py:183
  57.1 37.1 %all-gather.7.cloned.1.call-done = bf16[1792,1024]{1,0:T(8,128)(2,1)} async-done(((bf16[224,1024]{1,0:T(8,128)(2,1)}), bf16[1792,1024]{1,0:T(8,128)(2,1)}) %all-gather.7.cloned.1.call-update) | async-done | bytes 3670032 | tf_op jit(solution)/shard_map/token_rows/all_gather | solution.py:184
  100.4 4.4 pick.1
  113.7 38.8 %collective-permute-done.4 = bf16[1024,512]{1,0:T(8,128)(2,1)} collective-permute-done((bf16[1024,512]{1,0:T(8,128)(2,1)}, bf16[1024,512]{1,0:T(8,128)(2,1)}, u32[]{:S(2)}, u32[]{:S(2)}) %collective-permute-start.4) | collective-permute-done | bytes 1048608 | tf_op jit(solution)/shard_map/weights/ppermute | solution.py:125
  153.8 24.9 %collective-permute-done.5 = bf16[1024,512]{1,0:T(8,128)(2,1)} collective-permute-done((bf16[1024,512]{1,0:T(8,128)(2,1)}, bf16[1024,512]{1,0:T(8,128)(2,1)}, u32[]{:S(2)}, u32[]{:S(2)}) %collective-permute-start.5) | collective-permute-done | bytes 1048608 | tf_op jit(solution)/shard_map/weights/ppermute | solution.py:125
  187.0 23.7 %collective-permute-start.12 = (bf16[1792,256]{0,1:T(8,128)(2,1)}, bf16[1792,256]{0,1:T(8,128)(2,1)}, u32[]{:S(2)}, u32[]{:S(2)}) collective-permute-start(bf16[1792,256]{0,1:T(8,128)(2,1)} %convolution_convert_fusion.2), channel_id=1, source_target_pairs={{0,8},{1,9},{2,10},{3,11},{4,12},{5,13},{6,14},{7,15}} | collective-permute-start | bytes 2752520 | tf_op jit(solution)/shard_map/hidden_grad/ppermute | solution.py:136
  217.2 18.6 %collective-permute-done.11 = s32[8,56]{1,0:T(8,128)S(1)} collective-permute-done((s32[8,56]{1,0:T(8,128)S(1)}, s32[8,56]{1,0:T(8,128)S(1)}, u32[]{:S(2)}, u32[]{:S(2)}) %collective-permute-start.11) | collective-permute-done | bytes 1824 | tf_op jit(solution)/shard_map/grad_rows/ppermute | solution.py:125
  235.9 4.6 fusion.35
  250.1 12.1 %fusion = f32[1792,1024]{0,1:T(8,128)S(1)} fusion(bf16[1792,2048]{1,0:T(8,128)(2,1)} %all-gather.9.cloned.1.call-done, bf16[2048,512]{1,0:T(8,128)(2,1)} %collective-permute-done.7, bf16[2048,512]{1,0:T(8,128)(2,1)} %get-tuple-element.21), kind=kOutput, calls=%fused_computation.5 | convolution fusion | flops 7524581376 | bytes 18874368 | tf_op jit(solution)/shard_map/elementwise/dot_general | solution.py:18
  272.4 13.3 %collective-permute-done.14 = bf16[1792,256]{0,1:T(8,128)(2,1)S(1)} collective-permute-done((bf16[1792,256]{0,1:T(8,128)(2,1)S(1)}, bf16[1792,256]{0,1:T(8,128)(2,1)S(1)}, u32[]{:S(2)}, u32[]{:S(2)}) %collective-permute-start.14) | collective-permute-done | bytes 917536 | tf_op jit(solution)/shard_map/hidden_grad/ppermute | solution.py:136
  285.7 5.6 %collective-permute-done.17 = bf16[1792,256]{0,1:T(8,128)(2,1)S(1)} collective-permute-done((bf16[1792,256]{0,1:T(8,128)(2,1)S(1)}, bf16[1792,256]{0,1:T(8,128)(2,1)S(1)}, u32[]{:S(2)}, u32[]{:S(2)}) %collective-permute-start.17) | collective-permute-done | bytes 917536 | tf_op jit(solution)/shard_map/hidden_grad/ppermute | solution.py:137
  304.6 6.0 %copy.26 = bf16[1792,1024]{1,0:T(8,128)(2,1)} copy(bf16[1792,1024]{0,1:T(8,128)(2,1)} %pad_maximum_fusion.2) | data formatting | bytes 7340032 | tf_op jit(solution)/shard_map/input_grad/concatenate | solution.py:228
  313.1 4.6 fusion.9
  319.2 4.6 fusion.8
  324.3 35.8 %collective-permute-done.19 = bf16[896,1024]{1,0:T(8,128)(2,1)} collective-permute-done((bf16[896,1024]{1,0:T(8,128)(2,1)}, bf16[896,1024]{1,0:T(8,128)(2,1)}, u32[]{:S(2)}, u32[]{:S(2)}) %collective-permute-start.19) | collective-permute-done | bytes 1835040 | tf_op jit(solution)/shard_map/input_grad/ppermute | solution.py:150
  370.0 7.6 %convolution_convert_fusion = bf16[1792,1024]{1,0:T(8,128)(2,1)} fusion(bf16[1792,1024]{0,1:T(8,128)(2,1)} %all-gather.11.cloned.1.call-done, bf16[1024,1024]{1,0:T(8,128)(2,1)S(1)} %get-tuple-element.16), kind=kOutput, calls=%fused_computation.6 | convolution fusion | flops 3759931392 | bytes 9437184 | tf_op jit(solution)/shard_map/layer_out/dot_general | solution.py:18
  395.8 7.4 %collective-permute-done.23 = bf16[2,56,2048]{2,1,0:T(8,128)(2,1)S(1)} collective-permute-done((bf16[2,56,2048]{2,1,0:T(8,128)(2,1)S(1)}, bf16[2,56,2048]{2,1,0:T(8,128)(2,1)S(1)}, u32[]{:S(2)}, u32[]{:S(2)}) %collective-permute-start.23) | collective-permute-done | bytes 458784 | tf_op jit(solution)/shard_map/input_grad/ppermute | solution.py:136
  403.3 4.4 collective-permute-start.24
  407.8 7.2 %collective-permute-done.24 = bf16[2,56,2048]{2,1,0:T(8,128)(2,1)S(1)} collective-permute-done((bf16[2,56,2048]{2,1,0:T(8,128)(2,1)S(1)}, bf16[2,56,2048]{2,1,0:T(8,128)(2,1)S(1)}, u32[]{:S(2)}, u32[]{:S(2)}) %collective-permute-start.24) | collective-permute-done | bytes 458784 | tf_op jit(solution)/shard_map/input_grad/ppermute | solution.py:136
  416.0 5.0 %collective-permute-start.25 = (bf16[2,56,2048]{2,1,0:T(8,128)(2,1)S(1)}, bf16[2,56,2048]{2,1,0:T(8,128)(2,1)S(1)}, u32[]{:S(2)}, u32[]{:S(2)}) collective-permute-start(bf16[2,56,2048]{2,1,0:T(8,128)(2,1)S(1)} %get-tuple-element.23), channel_id=1, source_target_pairs={{0,8},{8,16},{16,24},{1,9},{9,17},{17,25},{2,10},{10,18},{18,26},{... | collective-permute-start | bytes 1376264 | tf_op jit(solution)/shard_map/input_grad/ppermute | solution.py:136
  422.5 4.9 %collective-permute-done.25 = bf16[2,56,2048]{2,1,0:T(8,128)(2,1)S(1)} collective-permute-done((bf16[2,56,2048]{2,1,0:T(8,128)(2,1)S(1)}, bf16[2,56,2048]{2,1,0:T(8,128)(2,1)S(1)}, u32[]{:S(2)}, u32[]{:S(2)}) %collective-permute-start.25) | collective-permute-done | bytes 458784 | tf_op jit(solution)/shard_map/input_grad/ppermute | solution.py:136
  427.4 9.6 %collective-permute-done.28 = bf16[2,56,2048]{2,1,0:T(8,128)(2,1)S(1)} collective-permute-done((bf16[2,56,2048]{2,1,0:T(8,128)(2,1)S(1)}, bf16[2,56,2048]{2,1,0:T(8,128)(2,1)S(1)}, u32[]{:S(2)}, u32[]{:S(2)}) %collective-permute-start.28) | collective-permute-done | bytes 458784 | tf_op jit(solution)/shard_map/input_grad/ppermute | solution.py:137
  442.9 13.1 %all-to-all-done = bf16[4,56,1024]{2,1,0:T(8,128)(2,1)S(1)} async-done(((bf16[4,56,1024]{2,1,0:T(8,128)(2,1)}), bf16[4,56,1024]{2,1,0:T(8,128)(2,1)S(1)}, u32[]{:S(2)}, u32[]{:S(2)}) %all-to-all-start) | async-done | bytes 458784 | tf_op jit(solution)/shard_map/layer_out/all_to_all | solution.py:223
  (146 shorter events, 117.0 us)
Async XLA Ops:
  7.2 49.9 %all-gather.5.cloned.1.call-start = ((), (), s32[]{:S(2)}) async-start(), calls=%async_computation.2 | async-start | bytes 2293760 | tf_op jit(solution)/shard_map/token_rows/all_gather | solution.py:183
  10.8 83.4 %all-gather.7.cloned.1.call-start = ((), (), s32[]{:S(2)}) async-start(), calls=%async_computation.3 | async-start | bytes 4128768 | tf_op jit(solution)/shard_map/token_rows/all_gather | solution.py:184
  28.5 221.6 %all-gather.9.cloned.1.call-start = ((), (), s32[]{:S(2)}) async-start(), calls=%async_computation.4 | async-start | bytes 9175040 | tf_op jit(solution)/shard_map/token_rows/all_gather | solution.py:187
  94.2 275.8 %all-gather.11.cloned.1.call-start = ((), (), s32[]{:S(2)}) async-start(), calls=%async_computation.5 | async-start | bytes 4587520 | tf_op jit(solution)/shard_map/layer_out/all_gather | solution.py:220
  104.8 47.6 %collective-permute-start.4 = (bf16[1024,512]{1,0:T(8,128)(2,1)}, bf16[1024,512]{1,0:T(8,128)(2,1)}, u32[]{:S(2)}, u32[]{:S(2)}) collective-permute-start(bf16[1024,512]{1,0:T(8,128)(2,1)} %get-tuple-element.12), channel_id=1, source_target_pairs={{0,8},{8,0},{16,24},{24,16},{1,9},{9,1},{17,25},{25,17},{2,10},{10... | collective-permute-start | bytes 3145736 | tf_op jit(solution)/shard_map/weights/ppermute | solution.py:125
  106.4 72.3 %collective-permute-start.5 = (bf16[1024,512]{1,0:T(8,128)(2,1)}, bf16[1024,512]{1,0:T(8,128)(2,1)}, u32[]{:S(2)}, u32[]{:S(2)}) collective-permute-start(bf16[1024,512]{1,0:T(8,128)(2,1)} %get-tuple-element.13), channel_id=1, source_target_pairs={{0,16},{8,24},{16,0},{24,8},{1,17},{9,25},{17,1},{25,9},{2,18},{10... | collective-permute-start | bytes 3145736 | tf_op jit(solution)/shard_map/weights/ppermute | solution.py:125
  108.8 71.2 %collective-permute-start.6 = (bf16[1024,512]{1,0:T(8,128)(2,1)}, bf16[1024,512]{1,0:T(8,128)(2,1)}, u32[]{:S(2)}, u32[]{:S(2)}) collective-permute-start(bf16[1024,512]{1,0:T(8,128)(2,1)} %get-tuple-element.14), channel_id=1, source_target_pairs={{0,24},{8,16},{16,8},{24,0},{1,25},{9,17},{17,9},{25,1},{2,26},{10... | collective-permute-start | bytes 3145736 | tf_op jit(solution)/shard_map/weights/ppermute | solution.py:125
  109.4 105.1 %collective-permute-start.9 = (s32[8,56]{1,0:T(8,128)S(1)}, s32[8,56]{1,0:T(8,128)S(1)}, u32[]{:S(2)}, u32[]{:S(2)}) collective-permute-start(s32[8,56]{1,0:T(8,128)S(1)} %reshape.102), channel_id=1, source_target_pairs={{0,8},{8,0},{16,24},{24,16},{1,9},{9,1},{17,25},{25,17},{2,10},{10... | collective-permute-start | bytes 5384 | tf_op jit(solution)/shard_map/grad_rows/ppermute | solution.py:125
  110.0 107.2 %collective-permute-start.10 = (s32[8,56]{1,0:T(8,128)S(1)}, s32[8,56]{1,0:T(8,128)S(1)}, u32[]{:S(2)}, u32[]{:S(2)}) collective-permute-start(s32[8,56]{1,0:T(8,128)S(1)} %reshape.102), channel_id=1, source_target_pairs={{0,16},{8,24},{16,0},{24,8},{1,17},{9,25},{17,1},{25,9},{2,18},{10... | collective-permute-start | bytes 5384 | tf_op jit(solution)/shard_map/grad_rows/ppermute | solution.py:125
  183.8 66.3 %collective-permute-start.7 = (bf16[2048,512]{1,0:T(8,128)(2,1)}, bf16[2048,512]{1,0:T(8,128)(2,1)}, u32[]{:S(2)}, u32[]{:S(2)}) collective-permute-start(bf16[2048,512]{1,0:T(8,128)(2,1)} %get-tuple-element.22), channel_id=1, source_target_pairs={{0,1},{1,0},{2,3},{3,2},{4,5},{5,4},{6,7},{7,6},{8,9},{9,8},{10,11... | collective-permute-start | bytes 6291464 | tf_op jit(solution)/shard_map/twin_weights/ppermute | solution.py:198
  187.0 53.5 %collective-permute-start.12 = (bf16[1792,256]{0,1:T(8,128)(2,1)}, bf16[1792,256]{0,1:T(8,128)(2,1)}, u32[]{:S(2)}, u32[]{:S(2)}) collective-permute-start(bf16[1792,256]{0,1:T(8,128)(2,1)} %convolution_convert_fusion.2), channel_id=1, source_target_pairs={{0,8},{1,9},{2,10},{3,11},{4,12},{5,13},{6,14},{7,15}} | collective-permute-start | bytes 2752520 | tf_op jit(solution)/shard_map/hidden_grad/ppermute | solution.py:136
  212.8 32.4 %collective-permute-start.15 = (bf16[1792,256]{0,1:T(8,128)(2,1)}, bf16[1792,256]{0,1:T(8,128)(2,1)}, u32[]{:S(2)}, u32[]{:S(2)}) collective-permute-start(bf16[1792,256]{0,1:T(8,128)(2,1)} %convolution_convert_fusion.1), channel_id=1, source_target_pairs={{24,16},{25,17},{26,18},{27,19},{28,20},{29,21},{30,22},{31,23}} | collective-permute-start | bytes 2752520 | tf_op jit(solution)/shard_map/hidden_grad/ppermute | solution.py:137
  214.5 21.3 %collective-permute-start.11 = (s32[8,56]{1,0:T(8,128)S(1)}, s32[8,56]{1,0:T(8,128)S(1)}, u32[]{:S(2)}, u32[]{:S(2)}) collective-permute-start(s32[8,56]{1,0:T(8,128)S(1)} %reshape.102), channel_id=1, source_target_pairs={{0,24},{8,16},{16,8},{24,0},{1,25},{9,17},{17,9},{25,1},{2,26},{10... | collective-permute-start | bytes 5384 | tf_op jit(solution)/shard_map/grad_rows/ppermute | solution.py:125
  243.9 21.6 %collective-permute-start.13 = (bf16[1792,256]{0,1:T(8,128)(2,1)}, bf16[1792,256]{0,1:T(8,128)(2,1)S(1)}, u32[]{:S(2)}, u32[]{:S(2)}) collective-permute-start(bf16[1792,256]{0,1:T(8,128)(2,1)} %add_convert_fusion.5), channel_id=1, source_target_pairs={{0,8},{8,16},{1,9},{9,17},{2,10},{10,18},{3,11},{11,19},{4,12},{12... | collective-permute-start | bytes 2752520 | tf_op jit(solution)/shard_map/hidden_grad/ppermute | solution.py:136
  248.5 19.7 %collective-permute-start.16 = (bf16[1792,256]{0,1:T(8,128)(2,1)}, bf16[1792,256]{0,1:T(8,128)(2,1)}, u32[]{:S(2)}, u32[]{:S(2)}) collective-permute-start(bf16[1792,256]{0,1:T(8,128)(2,1)} %add_convert_fusion.3), channel_id=1, source_target_pairs={{16,8},{24,16},{17,9},{25,17},{18,10},{26,18},{19,11},{27,19},{20,... | collective-permute-start | bytes 2752520 | tf_op jit(solution)/shard_map/hidden_grad/ppermute | solution.py:137
  265.6 20.1 %collective-permute-start.14 = (bf16[1792,256]{0,1:T(8,128)(2,1)S(1)}, bf16[1792,256]{0,1:T(8,128)(2,1)S(1)}, u32[]{:S(2)}, u32[]{:S(2)}) collective-permute-start(bf16[1792,256]{0,1:T(8,128)(2,1)S(1)} %add_convert_fusion.4), channel_id=1, source_target_pairs={{0,8},{8,16},{16,24},{1,9},{9,17},{17,25},{2,10},{10,18},{18,26},{... | collective-permute-start | bytes 2752520 | tf_op jit(solution)/shard_map/hidden_grad/ppermute | solution.py:136
  269.6 21.7 %collective-permute-start.17 = (bf16[1792,256]{0,1:T(8,128)(2,1)S(1)}, bf16[1792,256]{0,1:T(8,128)(2,1)S(1)}, u32[]{:S(2)}, u32[]{:S(2)}) collective-permute-start(bf16[1792,256]{0,1:T(8,128)(2,1)S(1)} %add_convert_fusion.2), channel_id=1, source_target_pairs={{8,0},{16,8},{24,16},{9,1},{17,9},{25,17},{10,2},{18,10},{26,18},{... | collective-permute-start | bytes 2752520 | tf_op jit(solution)/shard_map/hidden_grad/ppermute | solution.py:137
  294.3 144.2 %reduce-scatter.2.cloned.1.call-start = ((), (), s32[]{:S(2)}) async-start(), calls=%async_computation.6 | async-start | bytes 4128768 | tf_op jit(solution)/shard_map/layer_out/reduce_scatter | solution.py:222
  317.7 42.4 %collective-permute-start.19 = (bf16[896,1024]{1,0:T(8,128)(2,1)}, bf16[896,1024]{1,0:T(8,128)(2,1)}, u32[]{:S(2)}, u32[]{:S(2)}) collective-permute-start(bf16[896,1024]{1,0:T(8,128)(2,1)} %fusion.9), channel_id=1, source_target_pairs={{0,2},{1,3},{2,0},{3,1},{4,6},{5,7},{6,4},{7,5},{8,10},{9,11},{10,... | collective-permute-start | bytes 5505032 | tf_op jit(solution)/shard_map/input_grad/ppermute | solution.py:150
  323.8 42.1 %collective-permute-start.21 = (bf16[896,1024]{1,0:T(8,128)(2,1)}, bf16[896,1024]{1,0:T(8,128)(2,1)}, u32[]{:S(2)}, u32[]{:S(2)}) collective-permute-start(bf16[896,1024]{1,0:T(8,128)(2,1)} %fusion.8), channel_id=1, source_target_pairs={{0,4},{1,5},{2,6},{3,7},{4,0},{5,1},{6,2},{7,3},{8,12},{9,13},{10,... | collective-permute-start | bytes 5505032 | tf_op jit(solution)/shard_map/input_grad/ppermute | solution.py:150
  364.2 21.9 %collective-permute-start.20 = (bf16[448,1024]{1,0:T(8,128)(2,1)}, bf16[448,1024]{1,0:T(8,128)(2,1)}, u32[]{:S(2)}, u32[]{:S(2)}) collective-permute-start(bf16[448,1024]{1,0:T(8,128)(2,1)} %add_convert_fusion.1), channel_id=1, source_target_pairs={{0,4},{1,5},{2,6},{3,7},{4,0},{5,1},{6,2},{7,3},{8,12},{9,13},{10,... | collective-permute-start | bytes 2752520 | tf_op jit(solution)/shard_map/input_grad/ppermute | solution.py:150
  369.5 21.4 %collective-permute-start.22 = (bf16[448,1024]{1,0:T(8,128)(2,1)}, bf16[448,1024]{1,0:T(8,128)(2,1)S(1)}, u32[]{:S(2)}, u32[]{:S(2)}) collective-permute-start(bf16[448,1024]{1,0:T(8,128)(2,1)} %add_convert_fusion), channel_id=1, source_target_pairs={{0,2},{1,3},{2,0},{3,1},{4,6},{5,7},{6,4},{7,5},{8,10},{9,11},{10,... | collective-permute-start | bytes 2752520 | tf_op jit(solution)/shard_map/input_grad/ppermute | solution.py:150
  421.2 15.9 %collective-permute-start.28 = (bf16[2,56,2048]{2,1,0:T(8,128)(2,1)S(1)}, bf16[2,56,2048]{2,1,0:T(8,128)(2,1)S(1)}, u32[]{:S(2)}, u32[]{:S(2)}) collective-permute-start(bf16[2,56,2048]{2,1,0:T(8,128)(2,1)S(1)} %fusion.11), channel_id=1, source_target_pairs={{8,0},{16,8},{24,16},{9,1},{17,9},{25,17},{10,2},{18,10},{26,18},{... | collective-permute-start | bytes 1376264 | tf_op jit(solution)/shard_map/input_grad/ppermute | solution.py:137
  438.5 17.4 %all-to-all-start = ((bf16[4,56,1024]{2,1,0:T(8,128)(2,1)}), bf16[4,56,1024]{2,1,0:T(8,128)(2,1)S(1)}, u32[]{:S(2)}, u32[]{:S(2)}) async-start(bf16[4,56,1024]{2,1,0:T(8,128)(2,1)} %bitcast.111), calls=%async_computation.1 | async-start | bytes 917504 | tf_op jit(solution)/shard_map/layer_out/all_to_all | solution.py:223
  (28 other events, 297.9 us)
Sparse Core Ops, SparseCore 0:
  11.0 46.1 all-gather.4
  59.6 34.5 all-gather.6
  96.1 78.8 all-gather.8
  294.4 69.4 all-gather.10
  377.7 46.1 reduce-scatter.1

commit v2 on v1

--- a/solution.py
+++ b/solution.py
@@ -16,6 +16,37 @@
 
 def dot(left, right):
     return jnp.dot(left, right, preferred_element_type=F32)
+
+
+def forward(gate_pre, up_pre, mask):
+    logistic = 1.0 / (1.0 + jnp.exp(-gate_pre))
+    activated = gate_pre * logistic * mask
+    return activated * up_pre, mask * up_pre * logistic * (1.0 + gate_pre * (1.0 - logistic)), activated
+
+
+def factor_kernel(own_ref, twin_ref, mask_ref, factor_ref):
+    q = mask_ref.shape[1]
+    gate_pre, up_pre = (own_ref[:, i * q : (i + 1) * q] + twin_ref[:, i * q : (i + 1) * q].astype(F32) for i in range(2))
+    _, factor_ref[:, :q], factor_ref[:, q:] = forward(gate_pre, up_pre, mask_ref[...])
+
+
+def factors(own, twin, mask):
+    rows, wide = own.shape
+    q = wide // 2
+    if q % 128:
+        pre = own + twin.astype(F32)
+        return jnp.concatenate(forward(pre[:, :q], pre[:, q:], mask)[1:], axis=1)
+    tile = rows // 4
+    block = lambda columns: pl.BlockSpec((tile, columns), lambda i: (i, 0))
+    return pl.pallas_call(
+        factor_kernel,
+        grid=(4,),
+        in_specs=[block(wide), block(wide), block(q)],
+        out_specs=block(wide),
+        out_shape=jax.ShapeDtypeStruct((rows, wide), F32),
+        compiler_params=pltpu.CompilerParams(vmem_limit_bytes=32 * 2**20),
+        cost_estimate=pl.CostEstimate(flops=0, bytes_accessed=300 * 2**20, transcendentals=0),
+    )(own, twin, mask)
 
 
 def pick_kernel(nf, kept, width, layer_ref, keep_ref, gate, up, down, *rest):
@@ -101,7 +132,8 @@
                 pltpu.SemaphoreType.DMA((3 * kept,)),
                 pltpu.SemaphoreType.DMA((nf + 1,)),
             ],
-            compiler_params=pltpu.CompilerParams(vmem_limit_bytes=32 * 2**20),
+            compiler_params=pltpu.CompilerParams(vmem_limit_bytes=56 * 2**20),
+            cost_estimate=pl.CostEstimate(flops=0, bytes_accessed=12 * deep * hidden, transcendentals=0),
         )(f.reshape(1), keep_mask, gate_weight, up_weight, down_weight)
         return out[:nf], out[nf], out[nf + 1]
     alive = jnp.max(keep_mask, axis=0)
@@ -117,17 +149,21 @@
     return sends, down_pick, jnp.take(keep_mask, chosen, axis=1)
 
 
-def from_layers(pieces, f):
-    n = len(pieces)
-    stacked = jnp.zeros((n, *pieces[0].shape), pieces[0].dtype)
+after = lax.optimization_barrier
+
+
+def across(piece, p, n):
+    return lax.ppermute(piece, "fsdp", [(i, i ^ p) for i in range(n)]) if p else piece
+
+
+def in_order(pieces, f):
+    stacked = jnp.zeros((len(pieces), *pieces[0].shape), pieces[0].dtype)
     for p, piece in enumerate(pieces):
-        if p:
-            piece = lax.ppermute(piece, "fsdp", [(i, i ^ p) for i in range(n)])
         stacked = lax.dynamic_update_index_in_dim(stacked, piece, f ^ p, 0)
     return stacked
 
 
-def line_scatter(unit, n, axis, me):
+def line_steps(unit, n, axis, me):
     up = down = None
     for k in range(1, n):
         ahead, behind = unit(jnp.clip(me + n - k, 0, n - 1)), unit(jnp.clip(me - n + k, 0, n - 1))
@@ -135,110 +171,190 @@
             ahead, behind = ahead + up.astype(F32), behind + down.astype(F32)
         up = lax.ppermute(ahead.astype(BF16), axis, [(i, i + 1) for i in range(k)])
         down = lax.ppermute(behind.astype(BF16), axis, [(i, i - 1) for i in range(n - k, n)])
+        up, down = yield up, down
     return unit(me) + up.astype(F32) + down.astype(F32)
 
 
-def layer_scatter(rows_of, weight, n, chip, order):
-    held = list(range(n))
-    got = {d: [] for d in held}
-    for bit in order:
-        sent = [d for d in held if d >> bit & 1]
-        held = [d for d in held if not d >> bit & 1]
-        part = dot_t(jnp.concatenate([rows_of(chip ^ d) for d in sent]), weight)
-        for piece in zip(*(got[d] for d in sent)):
-            part = part + jnp.concatenate(piece).astype(F32)
-        arrived = lax.ppermute(part.astype(BF16), "seq", [(i, i ^ (2 << bit)) for i in range(2 * n)])
-        for d, piece in zip(sent, jnp.split(arrived, len(sent))):
-            got[d ^ (1 << bit)].append(piece)
-    total = dot_t(rows_of(chip), weight)
-    for piece in got[0]:
+def layers_sum(unit, n, me):
+    arrived = [across(unit(me ^ p).astype(BF16), p, n) for p in range(1, n)]
+    arrived = yield arrived
+    total = unit(me)
+    for piece in arrived:
         total = total + piece.astype(F32)
     return total
+
+
+def finish(steps, arrived):
+    try:
+        while True:
+            arrived = steps.send(arrived)
+    except StopIteration as end:
+        return end.value
+
+
+def assemble_kernel(places, *refs):
+    out = refs[-1]
+    for row, column, part, first, count in places:
+        width = refs[part].shape[1]
+        out[pl.ds(row, count), pl.ds(column, width)] = refs[part][pl.ds(first, count), :]
+
+
+def assemble(arrays, places, shape):
+    if shape[0] * shape[1] > 2**23:
+        return jnp.concatenate(arrays)
+    return pl.pallas_call(
+        functools.partial(assemble_kernel, places),
+        in_specs=[pl.BlockSpec(memory_space=pltpu.VMEM)] * len(arrays),
+        out_specs=pl.BlockSpec(memory_space=pltpu.VMEM),
+        out_shape=jax.ShapeDtypeStruct(shape, BF16),
+        compiler_params=pltpu.CompilerParams(vmem_limit_bytes=32 * 2**20),
+    )(*arrays)
+
+
+def stack_rows(arrays):
+    rows, columns = arrays[0].shape
+    return assemble(arrays, [(d * rows, 0, d, 0, rows) for d in range(len(arrays))], (len(arrays) * rows, columns))
+
+
+def seq_gather(x, n):
+    return [x] + [lax.ppermute(x, "seq", [(i, i ^ d) for i in range(n)]) for d in range(1, n)]
+
+
+def layer_scatter(rows, weight, n):
+    pieces = jnp.split(rows, n)
+    count = n.bit_length() - 1
+    halves = jnp.split(weight, 2)
+    held = [list(range(n)) for _ in halves]
+    got = [{d: [] for d in range(n)} for _ in halves]
+    for step in range(count):
+        for side, bit in enumerate((step, count - 1 - step)):
+            sent = [d for d in held[side] if d >> bit & 1]
+            held[side] = [d for d in held[side] if not d >> bit & 1]
+            part = dot_t(jnp.concatenate([pieces[d] for d in sent]), halves[side])
+            for piece in zip(*(got[side][d] for d in sent)):
+                part = part + jnp.concatenate(piece).astype(F32)
+            arrived = lax.ppermute(part.astype(BF16), "seq", [(i, i ^ (2 << bit)) for i in range(2 * n)])
+            for d, piece in zip(sent, jnp.split(arrived, len(sent))):
+                got[side][d ^ (1 << bit)].append(piece)
+        got = yield got
+    totals = []
+    for side, half in enumerate(halves):
+        total = dot_t(pieces[0], half)
+        for piece in got[side][0]:
+            total = total + piece.astype(F32)
+        totals.append(total)
+    return jnp.concatenate(totals, axis=1)
 
 
 def local(nf, ns, tokens, grad_out, gate_weight, up_weight, down_weight, keep_mask, task_ids):
     f, s = lax.axis_index("fsdp"), lax.axis_index("seq")
     core, chip, chips = s & 1, s >> 1, ns // 2
     rows, wide = tokens.shape
-    deep = wide // nf
+    deep, half = wide // nf, wide // 2
     every = nf * ns * rows
     swap = [(i, i ^ 1) for i in range(ns)]
 
-    with jax.named_scope("grad_rows"):
-        ids = from_layers([task_ids.reshape(ns, rows)] * nf, f)
-        grads = from_layers([lax.dynamic_slice_in_dim(grad_out, (f ^ p) * deep, deep, 1) for p in range(nf)], f)
     with jax.named_scope("pick"):
         sends, down_pick, keep_pick = pick(nf, f, keep_mask, gate_weight, up_weight, down_weight)
     hidden_width = down_pick.shape[0]
     q = hidden_width // nf
 
-    with jax.named_scope("weights"):
-        weight = from_layers(sends, f).reshape(wide, 2 * q)
-
-    half = wide // 2
+    with jax.named_scope("grad_rows"):
+        extra = jnp.zeros((8 * deep,), BF16).at[: ns * rows].set(task_ids.astype(BF16)).reshape(8, deep)
+        pieces = [
+            jnp.concatenate([lax.dynamic_slice_in_dim(grad_out, (f ^ p) * deep, deep, 1), extra]) for p in range(nf)
+        ]
+        grads = in_order([across(piece, p, nf) for p, piece in enumerate(pieces)], f)
+        ids = grads[:, rows:].reshape(nf, 8 * deep)[:, : ns * rows].reshape(nf, chips, 2 * rows)
+        ids = ids.transpose(1, 0, 2).reshape(every)
+        grads, sends = after((grads[:, :rows].reshape(nf * rows, deep), sends))
+        got = [sends[0], *(across(sends[p], p, nf) for p in (1, 2))]
+        grads = seq_gather(grads, ns)
+
     with jax.named_scope("token_rows"):
         own_rows = lax.dynamic_slice_in_dim(tokens, core * half, half, 1)
         twin_rows = lax.ppermute(lax.dynamic_slice_in_dim(tokens, (1 - core) * half, half, 1), "seq", swap)
-        token_rows = jnp.where(core == 0, jnp.stack([own_rows, twin_rows]), jnp.stack([twin_rows, own_rows]))
-        token_rows = lax.all_gather(token_rows, "fsdp", axis=1, tiled=False)
-        grads = lax.all_gather(grads.reshape(nf * rows, deep), "seq", axis=0, tiled=True)
-        token_rows, grads = lax.optimization_barrier((token_rows, grads))
+        token_rows = jnp.where(
+            core == 0, jnp.concatenate([own_rows, twin_rows]), jnp.concatenate([twin_rows, own_rows])
+        )
+        token_rows = lax.all_gather(token_rows, "fsdp", axis=0, tiled=True)
+        token_rows, grads, got, sends = after((token_rows, grads, got, sends))
         same_core = [[i for i in range(ns) if i & 1 == c] for c in range(2)]
-        token_rows = lax.all_gather(
-            token_rows.reshape(2 * nf * rows, half), "seq", axis=0, tiled=True, axis_index_groups=same_core
-        )
+        token_rows = lax.all_gather(token_rows, "seq", axis=0, tiled=True, axis_index_groups=same_core)
 
     with jax.named_scope("hidden_grad"):
-        hidden_grad = line_scatter(
-            lambda j: dot_t(grads, lax.dynamic_slice_in_dim(down_pick, j * q, q, 0)), nf, "fsdp", f
-        )
-
-    with jax.named_scope("twin_weights"):
+        got += [across(sends[p], p, nf) for p in range(3, nf)]
+        part = dot_t(stack_rows(grads[::2] + grads[1::2]), down_pick)
+        steps = line_steps(lambda j: lax.dynamic_slice_in_dim(part, j * q, q, 1), nf, "fsdp", f)
+        arrived, got = after((next(steps), got))
+
+    with jax.named_scope("weights"):
+        weight = in_order(got, f).reshape(wide, 2 * q)
         mine = lax.dynamic_slice_in_dim(weight, core * half, half, 0)
         other = lax.ppermute(lax.dynamic_slice_in_dim(weight, (1 - core) * half, half, 0), "seq", swap)
         both_weight = jnp.concatenate([mine, other], axis=1)
 
     with jax.named_scope("mask"):
-        ids = ids.transpose(1, 0, 2).reshape(every)
         tasks, kept = keep_pick.shape
         onehot = (ids[:, None] == jnp.arange(tasks, dtype=jnp.int32)[None, :]).astype(BF16)
         keep_columns = jnp.repeat(keep_pick.astype(BF16), hidden_width // kept, axis=1)
         mask = dot(onehot, lax.dynamic_slice_in_dim(keep_columns, f * q, q, 1))
 
-    with jax.named_scope("elementwise"):
+    with jax.named_scope("forward"):
         pre = dot(token_rows, both_weight)
-        pre = pre[:, : 2 * q] + lax.ppermute(pre[:, 2 * q :].astype(BF16), "seq", swap).astype(F32)
-        gate_pre, up_pre = pre[:, :q], pre[:, q:]
-        logistic = jax.nn.sigmoid(gate_pre)
-        activated = gate_pre * logistic
-        hidden = (activated * up_pre * mask).astype(BF16)
-        masked_grad = hidden_grad * mask
-        gate_grad = (masked_grad * up_pre * logistic * (1.0 + gate_pre * (1.0 - logistic))).astype(BF16)
-        up_grad = (masked_grad * activated).astype(BF16)
+        arrived, pre = after((steps.send(arrived), pre))
+        own, twin = pre[:, : 2 * q], lax.ppermute(pre[:, 2 * q :].astype(BF16), "seq", swap)
+        pre = own + twin.astype(F32)
+        hidden = forward(pre[:, :q], pre[:, q:], mask)[0]
+        hidden = hidden.astype(BF16).reshape(chips, nf, 2, rows, q).transpose(0, 2, 1, 3, 4).reshape(every, q)
+        hidden, own = after((hidden, own))
+        hidden_all = lax.all_gather(hidden, "fsdp", axis=1, tiled=True)
+        factor = factors(own, twin, mask)
+        if nf > 3:
+            arrived = steps.send(arrived)
+        factor = factor.reshape(chips, nf, 2, rows, 2 * q)
+        factor = jnp.stack([lax.dynamic_index_in_dim(factor, chip ^ d, 0, keepdims=False) for d in range(chips)])
+        arrived, factor = after((arrived, factor))
+        hidden_grad = finish(steps, arrived)
+
+    with jax.named_scope("input_grad"):
+        hidden_grad = hidden_grad.reshape(2, every // 2, q)
+        own = []
+        for c in range(2):
+            chunk = lax.dynamic_index_in_dim(hidden_grad, c ^ core, 0, keepdims=False)
+            scale = factor[:, :, c].reshape(every // 2, 2 * q)
+            own.append((scale * jnp.concatenate([chunk, chunk], axis=1)).astype(BF16))
+        both = [jnp.concatenate([own[c], lax.ppermute(own[c], "seq", swap)], axis=1) for c in range(2)]
+
+        def over_layers(part):
+            part = part.reshape(nf, rows, half)
+            return layers_sum(lambda j: lax.dynamic_index_in_dim(part, j, 0, keepdims=False), nf, f)
+
+        steps = chips.bit_length() - 1
+        first = layer_scatter(both[0], both_weight, chips)
+        arrived = next(first)
+        for _ in range(steps - 1):
+            arrived = first.send(arrived)
+        arrived, both[1] = after((arrived, both[1]))
+        second = layer_scatter(both[1], both_weight, chips)
+        waiting, hidden_all = after((next(second), hidden_all))
+        for _ in range(steps - 1):
+            waiting = second.send(waiting)
+        first = over_layers(finish(first, arrived))
+        arrived, waiting = after((next(first), waiting))
+        second = over_layers(finish(second, waiting))
+        totals = [finish(first, arrived).astype(BF16), finish(second, next(second)).astype(BF16)]
+        here = jnp.where(core == 0, totals[0], totals[1])
+        there = lax.ppermute(jnp.where(core == 0, totals[1], totals[0]), "seq", swap)
+        input_grad = jnp.where(
+            core == 0, jnp.concatenate([here, there], axis=1), jnp.concatenate([there, here], axis=1)
+        )
 
     with jax.named_scope("layer_out"):
-        hidden_all = lax.all_gather(hidden, "fsdp", axis=1, tiled=True)
         out_part = dot(hidden_all, down_pick).astype(BF16)
         out = lax.psum_scatter(out_part, "seq", scatter_dimension=0, tiled=True)
         out = lax.all_to_all(out.reshape(nf, rows, deep), "fsdp", 0, 0, tiled=False)
         layer_out = out.transpose(1, 0, 2).reshape(rows, wide)
-
-    with jax.named_scope("input_grad"):
-        own = jnp.concatenate([gate_grad, up_grad], axis=1)
-        both = jnp.concatenate([own, lax.ppermute(own, "seq", swap)], axis=1).reshape(chips, every // chips, 4 * q)
-        rows_of = lambda c: lax.dynamic_index_in_dim(both, c, 0, keepdims=False)
-        bits = list(range(chips.bit_length() - 1))
-        first = layer_scatter(rows_of, both_weight[: half // 2], chips, chip, bits)
-        second = layer_scatter(rows_of, both_weight[half // 2 :], chips, chip, bits[::-1])
-        part = jnp.concatenate([first, second], axis=1).reshape(2, nf, rows, half)
-        total = line_scatter(
-            lambda j: lax.dynamic_index_in_dim(part, j, 1, keepdims=False), nf, "fsdp", f
-        ).astype(BF16)
-        here = lax.dynamic_index_in_dim(total, core, 0, keepdims=False)
-        there = lax.ppermute(lax.dynamic_index_in_dim(total, 1 - core, 0, keepdims=False), "seq", swap)
-        input_grad = jnp.where(
-            core == 0, jnp.concatenate([here, there], axis=1), jnp.concatenate([there, here], axis=1)
-        )
     return layer_out, input_grad
 
 

time: 465 us -> 393 us (0.85)
  waiting for transfers between devices: 265 us -> 223 us
  matrix products: 63.1 us -> 37.8 us
  starting transfers between devices: 71 us -> 59 us
    all_gather x3 -> x2, waiting for transfers between devices: 65.6 us -> 18 us  [the longest x1 18 us: local(): lax.all_gather(token_rows, 'seq', axis=0, tiled=True, axis_index_groups=s...]
    dot_general x13, matrix products: 40.4 us -> 16.7 us  [dot_t(): lax.dot_general(left, right, (((1,), (1,)), ((), ())), preferred_element_...]
    ppermute x24 -> x29, starting transfers between devices: 62.7 us -> 45.1 us  [the longest x12 22.6 us: across(): lax.ppermute(piece, 'fsdp', [(i, i ^ p) for i in range(n)])]
    all_gather x1, waiting for transfers between devices: 0.01 us -> 6.61 us  [local(): hidden_all = lax.all_gather(hidden, 'fsdp', axis=1, tiled=True)]
    convert_element_type x6, other arithmetic: 3.36 us -> 9.7 us  [the longest x2 8.96 us: line_steps(): behind.astype(BF16)]
    concatenate x1 -> x0, local copies, waits for them, and re-layouts: 6.02 us -> none  [local(): jnp.concatenate([own, lax.ppermute(own, 'seq', swap)], axis=1)]
    ppermute x4 -> x8, starting transfers between devices: 3.88 us -> 9.3 us  [layer_scatter(): lax.ppermute(part.astype(BF16), 'seq', [(i, i ^ 2 << bit) for i in range(...]
    ppermute x24 -> x29, waiting for transfers between devices: 145 us -> 140 us  [the longest x12 64.9 us: across(): lax.ppermute(piece, 'fsdp', [(i, i ^ p) for i in range(n)])]
  transfers between devices with their start and end apart: 36 -> 44, of which waited for: 20 -> 26; matrix products, arithmetic and copies ran while one was open for 20% -> 15% of each run, Pallas kernels for 1% -> 2%
where the time goes in v2:
time: 393 us
  waiting for transfers between devices  223 us (57%)
  starting transfers between devices  59 us (15%)
  matrix products  37.8 us (10%)
  local copies, waits for them, and re-layouts  29 us (7%)
  other arithmetic  19.7 us (5%)
  between operations  14.6 us (4%)
  Pallas kernels  8.92 us (2%)
    ppermute x12, waiting for transfers between devices, across(): lax.ppermute(piece, 'fsdp', [(i, i ^ p) for i in range(n)])  64.9 us
    ppermute x8, waiting for transfers between devices, layer_scatter(): lax.ppermute(part.astype(BF16), 'seq', [(i, i ^ 2 << bit) for i in range(...  44.8 us
    ppermute x3, waiting for transfers between devices, line_steps(): up = lax.ppermute(ahead.astype(BF16), axis, [(i, i + 1) for i in range(k)])  34.7 us
    ppermute x7, waiting for transfers between devices, seq_gather(): lax.ppermute(x, 'seq', [(i, i ^ d) for i in range(n)])  33.7 us
    ppermute x12, starting transfers between devices, across(): lax.ppermute(piece, 'fsdp', [(i, i ^ p) for i in range(n)])  22.6 us
    dot_general x3, matrix products, dot(): return jnp.dot(left, right, preferred_element_type=F32)  21.1 us
    all_gather x1, waiting for transfers between devices, local(): lax.all_gather(token_rows, 'seq', axis=0, tiled=True, axis_index_groups=s...  18 us
    dot_general x13, matrix products, dot_t(): lax.dot_general(left, right, (((1,), (1,)), ((), ())), preferred_element_...  16.7 us
  transfers between devices with their start and end apart: 44, of which 26 were waited for; matrix products, arithmetic and copies ran while one was open for 15% of the time, Pallas kernels for 2%

profile of v2, /device:TPU:0, one launch (start us, length us, event | category | flops | bytes accessed | tf_op | source)
XLA Modules:
  0.0 392.6 jit_solution(9206047660827463177)
XLA Ops:
  16.7 7.5 %pick.1 = (bf16[1024,512]{1,0:T(8,128)(2,1)}, bf16[1024,512]{1,0:T(8,128)(2,1)}, bf16[1024,512]{1,0:T(8,128)(2,1)}, bf16[1024,512]{1,0:T(8,128)(2,1)}, bf16[1024,1024]{1,0:T(8,128)(2,1)}, /*index=5*/s32[8,8]{1,0:T(8,128)}) custom-call(s32[1]{0:T(128)} %bitcast.5.layer_ref, s32[8,14]{1,0:T(8,128)} %keep_ref.1, bf16[1024,1792]{1,0:T(8,128)(2,1)} %gate.1, ...), custom_call_target="tpu_custom_call" | custom-call | bytes 12582912 | tf_op jit(solution)/shard_map/pick/pallas_call | solution.py:122
  24.4 15.1 %collective-permute-done.2 = bf16[64,1024]{1,0:T(8,128)(2,1)S(1)} collective-permute-done((bf16[64,1024]{1,0:T(8,128)(2,1)S(1)}, bf16[64,1024]{1,0:T(8,128)(2,1)S(1)}, u32[]{:S(2)}, u32[]{:S(2)}) %collective-permute-start.2) | collective-permute-done | bytes 131104 | tf_op jit(solution)/shard_map/grad_rows/ppermute | solution.py:156
  55.0 8.3 %collective-permute-done.9.refs_3_ = bf16[224,1024]{1,0:T(8,128)(2,1)S(1)} collective-permute-done((bf16[224,1024]{1,0:T(8,128)(2,1)S(1)}, bf16[224,1024]{1,0:T(8,128)(2,1)S(1)}, u32[]{:S(2)}, u32[]{:S(2)}) %collective-permute-start.9) | collective-permute-done | bytes 458784 | tf_op jit(solution)/shard_map/grad_rows/ppermute | solution.py:220
  63.8 9.3 %collective-permute-done.8.refs_6_ = bf16[224,1024]{1,0:T(8,128)(2,1)S(1)} collective-permute-done((bf16[224,1024]{1,0:T(8,128)(2,1)S(1)}, bf16[224,1024]{1,0:T(8,128)(2,1)S(1)}, u32[]{:S(2)}, u32[]{:S(2)}) %collective-permute-start.8) | collective-permute-done | bytes 458784 | tf_op jit(solution)/shard_map/grad_rows/ppermute | solution.py:220
  73.7 9.2 %collective-permute-done.7.refs_2_ = bf16[224,1024]{1,0:T(8,128)(2,1)S(1)} collective-permute-done((bf16[224,1024]{1,0:T(8,128)(2,1)S(1)}, bf16[224,1024]{1,0:T(8,128)(2,1)S(1)}, u32[]{:S(2)}, u32[]{:S(2)}) %collective-permute-start.7) | collective-permute-done | bytes 458784 | tf_op jit(solution)/shard_map/grad_rows/ppermute | solution.py:220
  86.7 12.8 %collective-permute-done.11 = bf16[1024,512]{1,0:T(8,128)(2,1)S(1)} collective-permute-done((bf16[1024,512]{1,0:T(8,128)(2,1)S(1)}, bf16[1024,512]{1,0:T(8,128)(2,1)S(1)}, u32[]{:S(2)}, u32[]{:S(2)}) %collective-permute-start.11) | collective-permute-done | bytes 1048608 | tf_op jit(solution)/shard_map/grad_rows/ppermute | solution.py:156
  115.1 33.4 %collective-permute-done.13 = bf16[1792,256]{1,0:T(8,128)(2,1)S(1)} collective-permute-done((bf16[1792,256]{1,0:T(8,128)(2,1)S(1)}, bf16[1792,256]{1,0:T(8,128)(2,1)S(1)}, u32[]{:S(2)}, u32[]{:S(2)}) %collective-permute-start.13) | collective-permute-done | bytes 917536 | tf_op jit(solution)/shard_map/hidden_grad/ppermute | solution.py:172
  153.2 4.7 %add_convert_fusion.2 = (bf16[1792,256]{1,0:T(8,128)(2,1)}, bf16[1792,256]{1,0:T(8,128)(2,1)}) fusion(bf16[1792,256]{1,0:T(8,128)(2,1)S(1)} %collective-permute-done.14, f32[1792,1024]{1,0:T(8,128)} %copy-done.6, s32[]{:T(128)S(6)} %select_n.133, bf16[1792,256]{1,0:T(8,128)(2,1)} %copy-done.19, s32[]{:T(128)S(6)} %select_n.130), kind=kLoop, calls=%fused_computation.32 | loop fusion | flops 2752512 | bytes 7340040 | tf_op jit(solution)/shard_map/forward/convert_element_type | solution.py:173
  158.6 6.0 %collective-permute-start.16 = (bf16[1792,256]{1,0:T(8,128)(2,1)}, bf16[1792,256]{1,0:T(8,128)(2,1)}, u32[]{:S(2)}, u32[]{:S(2)}) collective-permute-start(bf16[1792,256]{1,0:T(8,128)(2,1)} %get-tuple-element.132), channel_id=1, source_target_pairs={{0,8},{8,16},{1,9},{9,17},{2,10},{10,18},{3,11},{11,19},{4,12},{12... | collective-permute-start | bytes 2752520 | tf_op jit(solution)/shard_map/forward/ppermute | solution.py:172
  164.7 18.0 %all-gather.6.cloned.1.call-done = bf16[1792,2048]{1,0:T(8,128)(2,1)} async-done(((bf16[448,2048]{1,0:T(8,128)(2,1)}), bf16[1792,2048]{1,0:T(8,128)(2,1)}) %all-gather.6.cloned.1.call-update) | async-done | bytes 7340048 | tf_op jit(solution)/shard_map/token_rows/all_gather | solution.py:283
  182.7 10.6 %fusion = f32[1792,1024]{1,0:T(8,128)S(1)} fusion(bf16[1792,2048]{1,0:T(8,128)(2,1)} %all-gather.6.cloned.1.call-done, bf16[2048,512]{1,0:T(8,128)(2,1)} %collective-permute-done.18, bf16[2048,512]{1,0:T(8,128)(2,1)S(1)} %get-tuple-element.138), kind=kOutput, calls=%fused_computation.5 | convolution fusion | flops 7524581376 | bytes 18874368 | tf_op jit(solution)/shard_map/forward/dot_general | solution.py:18
  204.6 5.6 %collective-permute-start.19 = (bf16[1792,256]{1,0:T(8,128)(2,1)}, bf16[1792,256]{1,0:T(8,128)(2,1)}, u32[]{:S(2)}, u32[]{:S(2)}) collective-permute-start(bf16[1792,256]{1,0:T(8,128)(2,1)} %get-tuple-element.130), channel_id=1, source_target_pairs={{0,8},{8,16},{16,24},{1,9},{9,17},{17,25},{2,10},{10,18},{18,26},{... | collective-permute-start | bytes 2752520 | tf_op jit(solution)/shard_map/forward/ppermute | solution.py:172
  221.4 6.7 %collective-permute-done.20 = bf16[1792,256]{1,0:T(8,128)(2,1)S(1)} collective-permute-done((bf16[1792,256]{1,0:T(8,128)(2,1)}, bf16[1792,256]{1,0:T(8,128)(2,1)S(1)}, u32[]{:S(2)}, u32[]{:S(2)}) %collective-permute-start.20) | collective-permute-done | bytes 917536 | tf_op jit(solution)/shard_map/forward/ppermute | solution.py:173
  242.0 17.9 %collective-permute-done.25 = bf16[448,1024]{1,0:T(8,128)(2,1)S(1)} collective-permute-done((bf16[448,1024]{1,0:T(8,128)(2,1)S(1)}, bf16[448,1024]{1,0:T(8,128)(2,1)S(1)}, u32[]{:S(2)}, u32[]{:S(2)}) %collective-permute-start.25) | collective-permute-done | bytes 917536 | tf_op jit(solution)/shard_map/input_grad/ppermute | solution.py:236
  265.1 7.2 %collective-permute-done.26 = bf16[224,1024]{1,0:T(8,128)(2,1)S(1)} collective-permute-done((bf16[224,1024]{1,0:T(8,128)(2,1)S(1)}, bf16[224,1024]{1,0:T(8,128)(2,1)S(1)}, u32[]{:S(2)}, u32[]{:S(2)}) %collective-permute-start.26) | collective-permute-done | bytes 458784 | tf_op jit(solution)/shard_map/input_grad/ppermute | solution.py:236
  278.7 16.2 %collective-permute-done.28 = bf16[448,1024]{1,0:T(8,128)(2,1)S(1)} collective-permute-done((bf16[448,1024]{1,0:T(8,128)(2,1)S(1)}, bf16[448,1024]{1,0:T(8,128)(2,1)S(1)}, u32[]{:S(2)}, u32[]{:S(2)}) %collective-permute-start.28) | collective-permute-done | bytes 917536 | tf_op jit(solution)/shard_map/input_grad/ppermute | solution.py:236
  297.7 6.6 %all-gather.8.cloned.1.call-done = bf16[1792,1024]{1,0:T(8,128)(2,1)} async-done(((bf16[1792,256]{1,0:T(8,128)(2,1)}), bf16[1792,1024]{1,0:T(8,128)(2,1)}) %all-gather.8.cloned.1.call-update) | async-done | bytes 3670032 | tf_op jit(solution)/shard_map/forward/all_gather | solution.py:311
  304.3 8.5 %convolution_convert_fusion = bf16[1792,1024]{1,0:T(8,128)(2,1)} fusion(bf16[1792,1024]{1,0:T(8,128)(2,1)} %all-gather.8.cloned.1.call-done, bf16[1024,1024]{1,0:T(8,128)(2,1)} %get-tuple-element.86), kind=kOutput, calls=%fused_computation.6 | convolution fusion | flops 3759931392 | bytes 9437184 | tf_op jit(solution)/shard_map/layer_out/dot_general | solution.py:18
  327.2 6.1 %collective-permute-done.32 = bf16[56,2048]{1,0:T(8,128)(2,1)S(1)} collective-permute-done((bf16[56,2048]{1,0:T(8,128)(2,1)S(1)}, bf16[56,2048]{1,0:T(8,128)(2,1)S(1)}, u32[]{:S(2)}, u32[]{:S(2)}) %collective-permute-start.32) | collective-permute-done | bytes 229408 | tf_op jit(solution)/shard_map/input_grad/ppermute | solution.py:156
  333.2 9.7 %collective-permute-done.31 = bf16[56,2048]{1,0:T(8,128)(2,1)S(1)} collective-permute-done((bf16[56,2048]{1,0:T(8,128)(2,1)S(1)}, bf16[56,2048]{1,0:T(8,128)(2,1)S(1)}, u32[]{:S(2)}, u32[]{:S(2)}) %collective-permute-start.31) | collective-permute-done | bytes 229408 | tf_op jit(solution)/shard_map/input_grad/ppermute | solution.py:156
  348.4 5.6 %collective-permute-done.35 = bf16[56,2048]{1,0:T(8,128)(2,1)S(1)} collective-permute-done((bf16[56,2048]{1,0:T(8,128)(2,1)S(1)}, bf16[56,2048]{1,0:T(8,128)(2,1)S(1)}, u32[]{:S(2)}, u32[]{:S(2)}) %collective-permute-start.35) | collective-permute-done | bytes 229408 | tf_op jit(solution)/shard_map/input_grad/ppermute | solution.py:156
  354.0 5.1 %collective-permute-done.37 = bf16[56,2048]{1,0:T(8,128)(2,1)S(1)} collective-permute-done((bf16[56,2048]{1,0:T(8,128)(2,1)S(1)}, bf16[56,2048]{1,0:T(8,128)(2,1)S(1)}, u32[]{:S(2)}, u32[]{:S(2)}) %collective-permute-start.37) | collective-permute-done | bytes 229408 | tf_op jit(solution)/shard_map/input_grad/ppermute | solution.py:156
  359.1 8.2 %collective-permute-done.36 = bf16[56,2048]{1,0:T(8,128)(2,1)S(1)} collective-permute-done((bf16[56,2048]{1,0:T(8,128)(2,1)S(1)}, bf16[56,2048]{1,0:T(8,128)(2,1)S(1)}, u32[]{:S(2)}, u32[]{:S(2)}) %collective-permute-start.36) | collective-permute-done | bytes 229408 | tf_op jit(solution)/shard_map/input_grad/ppermute | solution.py:156
  372.4 12.8 %all-to-all-done = bf16[4,56,1024]{2,1,0:T(8,128)(2,1)S(1)} async-done(((bf16[4,56,1024]{2,1,0:T(8,128)(2,1)}), bf16[4,56,1024]{2,1,0:T(8,128)(2,1)S(1)}, u32[]{:S(2)}, u32[]{:S(2)}) %all-to-all-start) | async-done | bytes 458784 | tf_op jit(solution)/shard_map/layer_out/all_to_all | solution.py:356
  (208 shorter events, 126.9 us)
Async XLA Ops:
  7.2 95.8 %all-gather.4.cloned.1.call-start = ((), (), s32[]{:S(2)}) async-start(), calls=%async_computation.2 | async-start | bytes 2293760 | tf_op jit(solution)/shard_map/token_rows/all_gather | solution.py:280
  10.9 171.8 %all-gather.6.cloned.1.call-start = ((), (), s32[]{:S(2)}) async-start(), calls=%async_computation.3 | async-start | bytes 9175040 | tf_op jit(solution)/shard_map/token_rows/all_gather | solution.py:283
  14.1 25.4 %collective-permute-start.3 = (bf16[64,1024]{1,0:T(8,128)(2,1)S(1)}, bf16[64,1024]{1,0:T(8,128)(2,1)S(1)}, u32[]{:S(2)}, u32[]{:S(2)}) collective-permute-start(bf16[64,1024]{1,0:T(8,128)(2,1)S(1)} %get-tuple-element.168), channel_id=1, source_target_pairs={{0,24},{8,16},{16,8},{24,0},{1,25},{9,17},{17,9},{25,1},{2,26},{10... | collective-permute-start | bytes 393224 | tf_op jit(solution)/shard_map/grad_rows/ppermute | solution.py:156
  16.6 22.9 %collective-permute-start.2 = (bf16[64,1024]{1,0:T(8,128)(2,1)S(1)}, bf16[64,1024]{1,0:T(8,128)(2,1)S(1)}, u32[]{:S(2)}, u32[]{:S(2)}) collective-permute-start(bf16[64,1024]{1,0:T(8,128)(2,1)S(1)} %get-tuple-element.170), channel_id=1, source_target_pairs={{0,16},{8,24},{16,0},{24,8},{1,17},{9,25},{17,1},{25,9},{2,18},{10... | collective-permute-start | bytes 393224 | tf_op jit(solution)/shard_map/grad_rows/ppermute | solution.py:156
  39.7 59.9 %collective-permute-start.11 = (bf16[1024,512]{1,0:T(8,128)(2,1)S(1)}, bf16[1024,512]{1,0:T(8,128)(2,1)S(1)}, u32[]{:S(2)}, u32[]{:S(2)}) collective-permute-start(bf16[1024,512]{1,0:T(8,128)(2,1)S(1)} %copy-done.30), channel_id=1, source_target_pairs={{0,8},{8,0},{16,24},{24,16},{1,9},{9,1},{17,25},{25,17},{2,10},{10... | collective-permute-start | bytes 3145736 | tf_op jit(solution)/shard_map/grad_rows/ppermute | solution.py:156
  42.5 60.5 %collective-permute-start.12 = (bf16[1024,512]{1,0:T(8,128)(2,1)S(1)}, bf16[1024,512]{1,0:T(8,128)(2,1)}, u32[]{:S(2)}, u32[]{:S(2)}) collective-permute-start(bf16[1024,512]{1,0:T(8,128)(2,1)S(1)} %copy-done.29), channel_id=1, source_target_pairs={{0,16},{8,24},{16,0},{24,8},{1,17},{9,25},{17,1},{25,9},{2,18},{10... | collective-permute-start | bytes 3145736 | tf_op jit(solution)/shard_map/grad_rows/ppermute | solution.py:156
  48.4 24.6 %collective-permute-start.8 = (bf16[224,1024]{1,0:T(8,128)(2,1)S(1)}, bf16[224,1024]{1,0:T(8,128)(2,1)S(1)}, u32[]{:S(2)}, u32[]{:S(2)}) collective-permute-start(bf16[224,1024]{1,0:T(8,128)(2,1)S(1)} %bitcast.103), channel_id=1, source_target_pairs={{0,5},{1,4},{2,7},{3,6},{4,1},{5,0},{6,3},{7,2},{8,13},{9,12},{10,... | collective-permute-start | bytes 1376264 | tf_op jit(solution)/shard_map/grad_rows/ppermute | solution.py:220
  53.2 29.6 %collective-permute-start.7 = (bf16[224,1024]{1,0:T(8,128)(2,1)S(1)}, bf16[224,1024]{1,0:T(8,128)(2,1)S(1)}, u32[]{:S(2)}, u32[]{:S(2)}) collective-permute-start(bf16[224,1024]{1,0:T(8,128)(2,1)S(1)} %bitcast.104), channel_id=1, source_target_pairs={{0,4},{1,5},{2,6},{3,7},{4,0},{5,1},{6,2},{7,3},{8,12},{9,13},{10,... | collective-permute-start | bytes 1376264 | tf_op jit(solution)/shard_map/grad_rows/ppermute | solution.py:220
  63.3 19.8 %collective-permute-start.6 = (bf16[224,1024]{1,0:T(8,128)(2,1)S(1)}, bf16[224,1024]{1,0:T(8,128)(2,1)S(1)}, u32[]{:S(2)}, u32[]{:S(2)}) collective-permute-start(bf16[224,1024]{1,0:T(8,128)(2,1)S(1)} %bitcast.105), channel_id=1, source_target_pairs={{0,3},{1,2},{2,1},{3,0},{4,7},{5,6},{6,5},{7,4},{8,11},{9,10},{10,... | collective-permute-start | bytes 1376264 | tf_op jit(solution)/shard_map/grad_rows/ppermute | solution.py:220
  103.0 201.2 %all-gather.8.cloned.1.call-start = ((), (), s32[]{:S(2)}) async-start(), calls=%async_computation.4 | async-start | bytes 4587520 | tf_op jit(solution)/shard_map/forward/all_gather | solution.py:311
  103.1 45.4 %collective-permute-start.15 = (bf16[1024,512]{1,0:T(8,128)(2,1)}, bf16[1024,512]{1,0:T(8,128)(2,1)S(1)}, u32[]{:S(2)}, u32[]{:S(2)}) collective-permute-start(bf16[1024,512]{1,0:T(8,128)(2,1)} %get-tuple-element.90), channel_id=1, source_target_pairs={{0,24},{8,16},{16,8},{24,0},{1,25},{9,17},{17,9},{25,1},{2,26},{10... | collective-permute-start | bytes 3145736 | tf_op jit(solution)/shard_map/hidden_grad/ppermute | solution.py:156
  113.4 35.0 %collective-permute-start.13 = (bf16[1792,256]{1,0:T(8,128)(2,1)S(1)}, bf16[1792,256]{1,0:T(8,128)(2,1)S(1)}, u32[]{:S(2)}, u32[]{:S(2)}) collective-permute-start(bf16[1792,256]{1,0:T(8,128)(2,1)S(1)} %get-tuple-element.134), channel_id=1, source_target_pairs={{0,8},{1,9},{2,10},{3,11},{4,12},{5,13},{6,14},{7,15}} | collective-permute-start | bytes 2752520 | tf_op jit(solution)/shard_map/hidden_grad/ppermute | solution.py:172
  157.9 35.4 %collective-permute-start.17 = (bf16[1792,256]{1,0:T(8,128)(2,1)}, bf16[1792,256]{1,0:T(8,128)(2,1)S(1)}, u32[]{:S(2)}, u32[]{:S(2)}) collective-permute-start(bf16[1792,256]{1,0:T(8,128)(2,1)} %get-tuple-element.131), channel_id=1, source_target_pairs={{16,8},{24,16},{17,9},{25,17},{18,10},{26,18},{19,11},{27,19},{20,... | collective-permute-start | bytes 2752520 | tf_op jit(solution)/shard_map/forward/ppermute | solution.py:173
  158.6 34.7 %collective-permute-start.16 = (bf16[1792,256]{1,0:T(8,128)(2,1)}, bf16[1792,256]{1,0:T(8,128)(2,1)}, u32[]{:S(2)}, u32[]{:S(2)}) collective-permute-start(bf16[1792,256]{1,0:T(8,128)(2,1)} %get-tuple-element.132), channel_id=1, source_target_pairs={{0,8},{8,16},{1,9},{9,17},{2,10},{10,18},{3,11},{11,19},{4,12},{12... | collective-permute-start | bytes 2752520 | tf_op jit(solution)/shard_map/forward/ppermute | solution.py:172
  203.3 24.9 %collective-permute-start.20 = (bf16[1792,256]{1,0:T(8,128)(2,1)}, bf16[1792,256]{1,0:T(8,128)(2,1)S(1)}, u32[]{:S(2)}, u32[]{:S(2)}) collective-permute-start(bf16[1792,256]{1,0:T(8,128)(2,1)} %get-tuple-element.129), channel_id=1, source_target_pairs={{8,0},{16,8},{24,16},{9,1},{17,9},{25,17},{10,2},{18,10},{26,18},{... | collective-permute-start | bytes 2752520 | tf_op jit(solution)/shard_map/forward/ppermute | solution.py:173
  204.6 24.9 %collective-permute-start.19 = (bf16[1792,256]{1,0:T(8,128)(2,1)}, bf16[1792,256]{1,0:T(8,128)(2,1)}, u32[]{:S(2)}, u32[]{:S(2)}) collective-permute-start(bf16[1792,256]{1,0:T(8,128)(2,1)} %get-tuple-element.130), channel_id=1, source_target_pairs={{0,8},{8,16},{16,24},{1,9},{9,17},{17,25},{2,10},{10,18},{18,26},{... | collective-permute-start | bytes 2752520 | tf_op jit(solution)/shard_map/forward/ppermute | solution.py:172
  231.1 136.6 %reduce-scatter.2.cloned.1.call-start = ((), (), s32[]{:S(2)}) async-start(), calls=%async_computation.5 | async-start | bytes 4128768 | tf_op jit(solution)/shard_map/layer_out/reduce_scatter | solution.py:355
  238.0 21.8 %collective-permute-start.25 = (bf16[448,1024]{1,0:T(8,128)(2,1)S(1)}, bf16[448,1024]{1,0:T(8,128)(2,1)S(1)}, u32[]{:S(2)}, u32[]{:S(2)}) collective-permute-start(bf16[448,1024]{1,0:T(8,128)(2,1)S(1)} %convolution_convert_fusion.3), channel_id=1, source_target_pairs={{0,4},{1,5},{2,6},{3,7},{4,0},{5,1},{6,2},{7,3},{8,12},{9,13},{10,... | collective-permute-start | bytes 2752520 | tf_op jit(solution)/shard_map/input_grad/ppermute | solution.py:236
  240.9 21.9 %collective-permute-start.23 = (bf16[448,1024]{1,0:T(8,128)(2,1)S(1)}, bf16[448,1024]{1,0:T(8,128)(2,1)S(1)}, u32[]{:S(2)}, u32[]{:S(2)}) collective-permute-start(bf16[448,1024]{1,0:T(8,128)(2,1)S(1)} %convolution_convert_fusion.4), channel_id=1, source_target_pairs={{0,2},{1,3},{2,0},{3,1},{4,6},{5,7},{6,4},{7,5},{8,10},{9,11},{10,... | collective-permute-start | bytes 2752520 | tf_op jit(solution)/shard_map/input_grad/ppermute | solution.py:236
  241.9 22.0 %collective-permute-start.27 = (bf16[896,512]{1,0:T(8,128)(2,1)S(1)}, bf16[896,512]{1,0:T(8,128)(2,1)S(1)}, u32[]{:S(2)}, u32[]{:S(2)}) collective-permute-start(bf16[896,512]{1,0:T(8,128)(2,1)S(1)} %fusion.5), channel_id=1, source_target_pairs={{0,1},{1,0},{2,3},{3,2},{4,5},{5,4},{6,7},{7,6},{8,9},{9,8},{10,11... | collective-permute-start | bytes 2752520 | tf_op jit(solution)/shard_map/input_grad/ppermute | solution.py:327
  318.6 24.3 %collective-permute-start.34 = (bf16[224,1024]{1,0:T(8,128)(2,1)S(1)}, bf16[224,1024]{1,0:T(8,128)(2,1)S(1)}, u32[]{:S(2)}, u32[]{:S(2)}) collective-permute-start(bf16[224,1024]{1,0:T(8,128)(2,1)S(1)} %fusion.13), channel_id=1, source_target_pairs={{0,2},{1,3},{2,0},{3,1},{4,6},{5,7},{6,4},{7,5},{8,10},{9,11},{10,... | collective-permute-start | bytes 1376264 | tf_op jit(solution)/shard_map/input_grad/ppermute | solution.py:236
  321.1 21.8 %collective-permute-start.33 = (bf16[224,1024]{1,0:T(8,128)(2,1)S(1)}, bf16[224,1024]{1,0:T(8,128)(2,1)S(1)}, u32[]{:S(2)}, u32[]{:S(2)}) collective-permute-start(bf16[224,1024]{1,0:T(8,128)(2,1)S(1)} %fusion.12), channel_id=1, source_target_pairs={{0,4},{1,5},{2,6},{3,7},{4,0},{5,1},{6,2},{7,3},{8,12},{9,13},{10,... | collective-permute-start | bytes 1376264 | tf_op jit(solution)/shard_map/input_grad/ppermute | solution.py:236
  323.0 19.9 %collective-permute-start.31 = (bf16[56,2048]{1,0:T(8,128)(2,1)S(1)}, bf16[56,2048]{1,0:T(8,128)(2,1)S(1)}, u32[]{:S(2)}, u32[]{:S(2)}) collective-permute-start(bf16[56,2048]{1,0:T(8,128)(2,1)S(1)} %get-tuple-element.149), channel_id=1, source_target_pairs={{0,16},{8,24},{16,0},{24,8},{1,17},{9,25},{17,1},{25,9},{2,18},{10... | collective-permute-start | bytes 688136 | tf_op jit(solution)/shard_map/input_grad/ppermute | solution.py:156
  323.2 19.7 %collective-permute-start.30 = (bf16[56,2048]{1,0:T(8,128)(2,1)S(1)}, bf16[56,2048]{1,0:T(8,128)(2,1)S(1)}, u32[]{:S(2)}, u32[]{:S(2)}) collective-permute-start(bf16[56,2048]{1,0:T(8,128)(2,1)S(1)} %get-tuple-element.150), channel_id=1, source_target_pairs={{0,8},{8,0},{16,24},{24,16},{1,9},{9,1},{17,25},{25,17},{2,10},{10... | collective-permute-start | bytes 688136 | tf_op jit(solution)/shard_map/input_grad/ppermute | solution.py:156
  (52 other events, 525.7 us)
Sparse Core Ops, SparseCore 0:
  11.0 70.5 all-gather.3
  103.2 79.4 all-gather.5
  231.2 73.0 all-gather.7
  312.9 46.9 reduce-scatter.1

commit v3 on v2

--- a/solution.py
+++ b/solution.py
@@ -284,8 +284,8 @@
 
     with jax.named_scope("hidden_grad"):
         got += [across(sends[p], p, nf) for p in range(3, nf)]
-        part = dot_t(stack_rows(grads[::2] + grads[1::2]), down_pick)
-        steps = line_steps(lambda j: lax.dynamic_slice_in_dim(part, j * q, q, 1), nf, "fsdp", f)
+        part = dot_t(stack_rows(grads[::2] + grads[1::2]), down_pick).astype(BF16)
+        steps = line_steps(lambda j: lax.dynamic_slice_in_dim(part, j * q, q, 1).astype(F32), nf, "fsdp", f)
         arrived, got = after((next(steps), got))
 
     with jax.named_scope("weights"):

time: 393 us -> 393 us (level)
    unnamed x66 -> x64, local copies, waits for them, and re-layouts: 15.3 us -> 16.2 us
where the time goes in v3:
time: 393 us; the launch traced here: 392 us
  waiting for transfers between devices  221 us (56%)
  starting transfers between devices  59.1 us (15%)
  matrix products  38.1 us (10%)
  local copies, waits for them, and re-layouts  29.9 us (8%)
  other arithmetic  20 us (5%)
  between operations  14.6 us (4%)
  Pallas kernels  8.9 us (2%)
    ppermute x12, waiting for transfers between devices, across(): lax.ppermute(piece, 'fsdp', [(i, i ^ p) for i in range(n)])  65 us
    ppermute x8, waiting for transfers between devices, layer_scatter(): lax.ppermute(part.astype(BF16), 'seq', [(i, i ^ 2 << bit) for i in range(...  45.2 us
    ppermute x3, waiting for transfers between devices, line_steps(): up = lax.ppermute(ahead.astype(BF16), axis, [(i, i + 1) for i in range(k)])  34.4 us
    ppermute x7, waiting for transfers between devices, seq_gather(): lax.ppermute(x, 'seq', [(i, i ^ d) for i in range(n)])  33.7 us
    ppermute x12, starting transfers between devices, across(): lax.ppermute(piece, 'fsdp', [(i, i ^ p) for i in range(n)])  22.6 us
    dot_general x3, matrix products, dot(): return jnp.dot(left, right, preferred_element_type=F32)  21.1 us
    all_gather x1, waiting for transfers between devices, local(): lax.all_gather(token_rows, 'seq', axis=0, tiled=True, axis_index_groups=s...  17.6 us
    dot_general x13, matrix products, dot_t(): lax.dot_general(left, right, (((1,), (1,)), ((), ())), preferred_element_...  17 us
  transfers between devices with their start and end apart: 44, of which 26 were waited for; matrix products, arithmetic and copies ran while one was open for 15% of the time, Pallas kernels for 2%

profile of v3, /device:TPU:0, one launch (start us, length us, event | category | flops | bytes accessed | tf_op | source)
XLA Modules:
  0.0 391.8 jit_solution(2858076579342881780)
XLA Ops:
  16.7 7.5 %pick.1 = (bf16[1024,512]{1,0:T(8,128)(2,1)}, bf16[1024,512]{1,0:T(8,128)(2,1)}, bf16[1024,512]{1,0:T(8,128)(2,1)}, bf16[1024,512]{1,0:T(8,128)(2,1)}, bf16[1024,1024]{1,0:T(8,128)(2,1)}, /*index=5*/s32[8,8]{1,0:T(8,128)}) custom-call(s32[1]{0:T(128)} %bitcast.5.layer_ref, s32[8,14]{1,0:T(8,128)} %keep_ref.1, bf16[1024,1792]{1,0:T(8,128)(2,1)} %gate.1, ...), custom_call_target="tpu_custom_call" | custom-call | bytes 12582912 | tf_op jit(solution)/shard_map/pick/pallas_call | solution.py:122
  24.4 15.1 %collective-permute-done.2 = bf16[64,1024]{1,0:T(8,128)(2,1)S(1)} collective-permute-done((bf16[64,1024]{1,0:T(8,128)(2,1)S(1)}, bf16[64,1024]{1,0:T(8,128)(2,1)S(1)}, u32[]{:S(2)}, u32[]{:S(2)}) %collective-permute-start.2) | collective-permute-done | bytes 131104 | tf_op jit(solution)/shard_map/grad_rows/ppermute | solution.py:156
  55.0 8.3 %collective-permute-done.9.refs_3_ = bf16[224,1024]{1,0:T(8,128)(2,1)S(1)} collective-permute-done((bf16[224,1024]{1,0:T(8,128)(2,1)S(1)}, bf16[224,1024]{1,0:T(8,128)(2,1)S(1)}, u32[]{:S(2)}, u32[]{:S(2)}) %collective-permute-start.9) | collective-permute-done | bytes 458784 | tf_op jit(solution)/shard_map/grad_rows/ppermute | solution.py:220
  63.8 9.3 %collective-permute-done.8.refs_6_ = bf16[224,1024]{1,0:T(8,128)(2,1)S(1)} collective-permute-done((bf16[224,1024]{1,0:T(8,128)(2,1)S(1)}, bf16[224,1024]{1,0:T(8,128)(2,1)S(1)}, u32[]{:S(2)}, u32[]{:S(2)}) %collective-permute-start.8) | collective-permute-done | bytes 458784 | tf_op jit(solution)/shard_map/grad_rows/ppermute | solution.py:220
  73.7 9.2 %collective-permute-done.7.refs_2_ = bf16[224,1024]{1,0:T(8,128)(2,1)S(1)} collective-permute-done((bf16[224,1024]{1,0:T(8,128)(2,1)S(1)}, bf16[224,1024]{1,0:T(8,128)(2,1)S(1)}, u32[]{:S(2)}, u32[]{:S(2)}) %collective-permute-start.7) | collective-permute-done | bytes 458784 | tf_op jit(solution)/shard_map/grad_rows/ppermute | solution.py:220
  86.7 12.8 %collective-permute-done.11 = bf16[1024,512]{1,0:T(8,128)(2,1)S(1)} collective-permute-done((bf16[1024,512]{1,0:T(8,128)(2,1)S(1)}, bf16[1024,512]{1,0:T(8,128)(2,1)S(1)}, u32[]{:S(2)}, u32[]{:S(2)}) %collective-permute-start.11) | collective-permute-done | bytes 1048608 | tf_op jit(solution)/shard_map/grad_rows/ppermute | solution.py:156
  115.4 33.1 %collective-permute-done.13 = bf16[1792,256]{1,0:T(8,128)(2,1)S(1)} collective-permute-done((bf16[1792,256]{1,0:T(8,128)(2,1)S(1)}, bf16[1792,256]{1,0:T(8,128)(2,1)S(1)}, u32[]{:S(2)}, u32[]{:S(2)}) %collective-permute-start.13) | collective-permute-done | bytes 917536 | tf_op jit(solution)/shard_map/hidden_grad/ppermute | solution.py:172
  159.2 5.9 %collective-permute-start.16 = (bf16[1792,256]{1,0:T(8,128)(2,1)}, bf16[1792,256]{1,0:T(8,128)(2,1)}, u32[]{:S(2)}, u32[]{:S(2)}) collective-permute-start(bf16[1792,256]{1,0:T(8,128)(2,1)} %get-tuple-element.142), channel_id=1, source_target_pairs={{0,8},{8,16},{1,9},{9,17},{2,10},{10,18},{3,11},{11,19},{4,12},{12... | collective-permute-start | bytes 2752520 | tf_op jit(solution)/shard_map/forward/ppermute | solution.py:172
  165.1 17.6 %all-gather.6.cloned.1.call-done = bf16[1792,2048]{1,0:T(8,128)(2,1)} async-done(((bf16[448,2048]{1,0:T(8,128)(2,1)}), bf16[1792,2048]{1,0:T(8,128)(2,1)}) %all-gather.6.cloned.1.call-update) | async-done | bytes 7340048 | tf_op jit(solution)/shard_map/token_rows/all_gather | solution.py:283
  182.7 10.6 %fusion = f32[1792,1024]{1,0:T(8,128)S(1)} fusion(bf16[1792,2048]{1,0:T(8,128)(2,1)} %all-gather.6.cloned.1.call-done, bf16[2048,512]{1,0:T(8,128)(2,1)} %collective-permute-done.18, bf16[2048,512]{1,0:T(8,128)(2,1)S(1)} %get-tuple-element.132), kind=kOutput, calls=%fused_computation.5 | convolution fusion | flops 7524581376 | bytes 18874368 | tf_op jit(solution)/shard_map/forward/dot_general | solution.py:18
  203.8 5.5 %collective-permute-start.19 = (bf16[1792,256]{1,0:T(8,128)(2,1)}, bf16[1792,256]{1,0:T(8,128)(2,1)}, u32[]{:S(2)}, u32[]{:S(2)}) collective-permute-start(bf16[1792,256]{1,0:T(8,128)(2,1)} %get-tuple-element.140), channel_id=1, source_target_pairs={{0,8},{8,16},{16,24},{1,9},{9,17},{17,25},{2,10},{10,18},{18,26},{... | collective-permute-start | bytes 2752520 | tf_op jit(solution)/shard_map/forward/ppermute | solution.py:172
  209.3 4.5 %fusion.56 = (f32[1792,512]{1,0:T(8,128)}, f32[1792,512]{1,0:T(8,128)S(1)}) fusion(f32[1792,1024]{1,0:T(8,128)} %copy-done.12, bf16[1792,512]{1,0:T(8,128)(2,1)S(1)} %collective-permute-done.21.twin_ref), kind=kLoop, calls=%fused_computation.138 | loop fusion | flops 1835008 | bytes 12845056 | tf_op jit(solution)/shard_map/forward/slice | solution.py:306
  222.6 4.8 %collective-permute-done.20 = bf16[1792,256]{1,0:T(8,128)(2,1)S(1)} collective-permute-done((bf16[1792,256]{1,0:T(8,128)(2,1)}, bf16[1792,256]{1,0:T(8,128)(2,1)S(1)}, u32[]{:S(2)}, u32[]{:S(2)}) %collective-permute-start.20) | collective-permute-done | bytes 917536 | tf_op jit(solution)/shard_map/forward/ppermute | solution.py:173
  240.7 18.1 %collective-permute-done.25 = bf16[448,1024]{1,0:T(8,128)(2,1)S(1)} collective-permute-done((bf16[448,1024]{1,0:T(8,128)(2,1)S(1)}, bf16[448,1024]{1,0:T(8,128)(2,1)S(1)}, u32[]{:S(2)}, u32[]{:S(2)}) %collective-permute-start.25) | collective-permute-done | bytes 917536 | tf_op jit(solution)/shard_map/input_grad/ppermute | solution.py:236
  264.0 7.2 %collective-permute-done.26 = bf16[224,1024]{1,0:T(8,128)(2,1)S(1)} collective-permute-done((bf16[224,1024]{1,0:T(8,128)(2,1)S(1)}, bf16[224,1024]{1,0:T(8,128)(2,1)S(1)}, u32[]{:S(2)}, u32[]{:S(2)}) %collective-permute-start.26) | collective-permute-done | bytes 458784 | tf_op jit(solution)/shard_map/input_grad/ppermute | solution.py:236
  277.9 16.6 %collective-permute-done.28 = bf16[448,1024]{1,0:T(8,128)(2,1)S(1)} collective-permute-done((bf16[448,1024]{1,0:T(8,128)(2,1)S(1)}, bf16[448,1024]{1,0:T(8,128)(2,1)S(1)}, u32[]{:S(2)}, u32[]{:S(2)}) %collective-permute-start.28) | collective-permute-done | bytes 917536 | tf_op jit(solution)/shard_map/input_grad/ppermute | solution.py:236
  297.1 6.4 %all-gather.8.cloned.1.call-done = bf16[1792,1024]{1,0:T(8,128)(2,1)} async-done(((bf16[1792,256]{1,0:T(8,128)(2,1)}), bf16[1792,1024]{1,0:T(8,128)(2,1)}) %all-gather.8.cloned.1.call-update) | async-done | bytes 3670032 | tf_op jit(solution)/shard_map/forward/all_gather | solution.py:311
  303.5 8.5 %convolution_convert_fusion = bf16[1792,1024]{1,0:T(8,128)(2,1)} fusion(bf16[1792,1024]{1,0:T(8,128)(2,1)} %all-gather.8.cloned.1.call-done, bf16[1024,1024]{1,0:T(8,128)(2,1)} %get-tuple-element.86), kind=kOutput, calls=%fused_computation.6 | convolution fusion | flops 3759931392 | bytes 9437184 | tf_op jit(solution)/shard_map/layer_out/dot_general | solution.py:18
  326.4 6.1 %collective-permute-done.32 = bf16[56,2048]{1,0:T(8,128)(2,1)S(1)} collective-permute-done((bf16[56,2048]{1,0:T(8,128)(2,1)S(1)}, bf16[56,2048]{1,0:T(8,128)(2,1)S(1)}, u32[]{:S(2)}, u32[]{:S(2)}) %collective-permute-start.32) | collective-permute-done | bytes 229408 | tf_op jit(solution)/shard_map/input_grad/ppermute | solution.py:156
  332.4 9.7 %collective-permute-done.31 = bf16[56,2048]{1,0:T(8,128)(2,1)S(1)} collective-permute-done((bf16[56,2048]{1,0:T(8,128)(2,1)S(1)}, bf16[56,2048]{1,0:T(8,128)(2,1)S(1)}, u32[]{:S(2)}, u32[]{:S(2)}) %collective-permute-start.31) | collective-permute-done | bytes 229408 | tf_op jit(solution)/shard_map/input_grad/ppermute | solution.py:156
  347.6 5.6 %collective-permute-done.35 = bf16[56,2048]{1,0:T(8,128)(2,1)S(1)} collective-permute-done((bf16[56,2048]{1,0:T(8,128)(2,1)S(1)}, bf16[56,2048]{1,0:T(8,128)(2,1)S(1)}, u32[]{:S(2)}, u32[]{:S(2)}) %collective-permute-start.35) | collective-permute-done | bytes 229408 | tf_op jit(solution)/shard_map/input_grad/ppermute | solution.py:156
  353.2 5.0 %collective-permute-done.37 = bf16[56,2048]{1,0:T(8,128)(2,1)S(1)} collective-permute-done((bf16[56,2048]{1,0:T(8,128)(2,1)S(1)}, bf16[56,2048]{1,0:T(8,128)(2,1)S(1)}, u32[]{:S(2)}, u32[]{:S(2)}) %collective-permute-start.37) | collective-permute-done | bytes 229408 | tf_op jit(solution)/shard_map/input_grad/ppermute | solution.py:156
  358.3 8.1 %collective-permute-done.36 = bf16[56,2048]{1,0:T(8,128)(2,1)S(1)} collective-permute-done((bf16[56,2048]{1,0:T(8,128)(2,1)S(1)}, bf16[56,2048]{1,0:T(8,128)(2,1)S(1)}, u32[]{:S(2)}, u32[]{:S(2)}) %collective-permute-start.36) | collective-permute-done | bytes 229408 | tf_op jit(solution)/shard_map/input_grad/ppermute | solution.py:156
  371.6 12.8 %all-to-all-done = bf16[4,56,1024]{2,1,0:T(8,128)(2,1)S(1)} async-done(((bf16[4,56,1024]{2,1,0:T(8,128)(2,1)}), bf16[4,56,1024]{2,1,0:T(8,128)(2,1)S(1)}, u32[]{:S(2)}, u32[]{:S(2)}) %all-to-all-start) | async-done | bytes 458784 | tf_op jit(solution)/shard_map/layer_out/all_to_all | solution.py:356
  (206 shorter events, 128.6 us)
Async XLA Ops:
  7.2 95.8 %all-gather.4.cloned.1.call-start = ((), (), s32[]{:S(2)}) async-start(), calls=%async_computation.2 | async-start | bytes 2293760 | tf_op jit(solution)/shard_map/token_rows/all_gather | solution.py:280
  10.9 171.8 %all-gather.6.cloned.1.call-start = ((), (), s32[]{:S(2)}) async-start(), calls=%async_computation.3 | async-start | bytes 9175040 | tf_op jit(solution)/shard_map/token_rows/all_gather | solution.py:283
  14.1 25.4 %collective-permute-start.3 = (bf16[64,1024]{1,0:T(8,128)(2,1)S(1)}, bf16[64,1024]{1,0:T(8,128)(2,1)S(1)}, u32[]{:S(2)}, u32[]{:S(2)}) collective-permute-start(bf16[64,1024]{1,0:T(8,128)(2,1)S(1)} %get-tuple-element.168), channel_id=1, source_target_pairs={{0,24},{8,16},{16,8},{24,0},{1,25},{9,17},{17,9},{25,1},{2,26},{10... | collective-permute-start | bytes 393224 | tf_op jit(solution)/shard_map/grad_rows/ppermute | solution.py:156
  16.6 22.9 %collective-permute-start.2 = (bf16[64,1024]{1,0:T(8,128)(2,1)S(1)}, bf16[64,1024]{1,0:T(8,128)(2,1)S(1)}, u32[]{:S(2)}, u32[]{:S(2)}) collective-permute-start(bf16[64,1024]{1,0:T(8,128)(2,1)S(1)} %get-tuple-element.170), channel_id=1, source_target_pairs={{0,16},{8,24},{16,0},{24,8},{1,17},{9,25},{17,1},{25,9},{2,18},{10... | collective-permute-start | bytes 393224 | tf_op jit(solution)/shard_map/grad_rows/ppermute | solution.py:156
  39.7 59.9 %collective-permute-start.11 = (bf16[1024,512]{1,0:T(8,128)(2,1)S(1)}, bf16[1024,512]{1,0:T(8,128)(2,1)S(1)}, u32[]{:S(2)}, u32[]{:S(2)}) collective-permute-start(bf16[1024,512]{1,0:T(8,128)(2,1)S(1)} %copy-done.29), channel_id=1, source_target_pairs={{0,8},{8,0},{16,24},{24,16},{1,9},{9,1},{17,25},{25,17},{2,10},{10... | collective-permute-start | bytes 3145736 | tf_op jit(solution)/shard_map/grad_rows/ppermute | solution.py:156
  42.5 60.5 %collective-permute-start.12 = (bf16[1024,512]{1,0:T(8,128)(2,1)S(1)}, bf16[1024,512]{1,0:T(8,128)(2,1)}, u32[]{:S(2)}, u32[]{:S(2)}) collective-permute-start(bf16[1024,512]{1,0:T(8,128)(2,1)S(1)} %copy-done.28), channel_id=1, source_target_pairs={{0,16},{8,24},{16,0},{24,8},{1,17},{9,25},{17,1},{25,9},{2,18},{10... | collective-permute-start | bytes 3145736 | tf_op jit(solution)/shard_map/grad_rows/ppermute | solution.py:156
  48.4 24.6 %collective-permute-start.8 = (bf16[224,1024]{1,0:T(8,128)(2,1)S(1)}, bf16[224,1024]{1,0:T(8,128)(2,1)S(1)}, u32[]{:S(2)}, u32[]{:S(2)}) collective-permute-start(bf16[224,1024]{1,0:T(8,128)(2,1)S(1)} %bitcast.103), channel_id=1, source_target_pairs={{0,5},{1,4},{2,7},{3,6},{4,1},{5,0},{6,3},{7,2},{8,13},{9,12},{10,... | collective-permute-start | bytes 1376264 | tf_op jit(solution)/shard_map/grad_rows/ppermute | solution.py:220
  53.2 29.6 %collective-permute-start.7 = (bf16[224,1024]{1,0:T(8,128)(2,1)S(1)}, bf16[224,1024]{1,0:T(8,128)(2,1)S(1)}, u32[]{:S(2)}, u32[]{:S(2)}) collective-permute-start(bf16[224,1024]{1,0:T(8,128)(2,1)S(1)} %bitcast.104), channel_id=1, source_target_pairs={{0,4},{1,5},{2,6},{3,7},{4,0},{5,1},{6,2},{7,3},{8,12},{9,13},{10,... | collective-permute-start | bytes 1376264 | tf_op jit(solution)/shard_map/grad_rows/ppermute | solution.py:220
  103.0 200.5 %all-gather.8.cloned.1.call-start = ((), (), s32[]{:S(2)}) async-start(), calls=%async_computation.4 | async-start | bytes 4587520 | tf_op jit(solution)/shard_map/forward/all_gather | solution.py:311
  103.1 45.4 %collective-permute-start.15 = (bf16[1024,512]{1,0:T(8,128)(2,1)}, bf16[1024,512]{1,0:T(8,128)(2,1)S(1)}, u32[]{:S(2)}, u32[]{:S(2)}) collective-permute-start(bf16[1024,512]{1,0:T(8,128)(2,1)} %get-tuple-element.90), channel_id=1, source_target_pairs={{0,24},{8,16},{16,8},{24,0},{1,25},{9,17},{17,9},{25,1},{2,26},{10... | collective-permute-start | bytes 3145736 | tf_op jit(solution)/shard_map/hidden_grad/ppermute | solution.py:156
  113.8 34.7 %collective-permute-start.13 = (bf16[1792,256]{1,0:T(8,128)(2,1)S(1)}, bf16[1792,256]{1,0:T(8,128)(2,1)S(1)}, u32[]{:S(2)}, u32[]{:S(2)}) collective-permute-start(bf16[1792,256]{1,0:T(8,128)(2,1)S(1)} %get-tuple-element.144), channel_id=1, source_target_pairs={{0,8},{1,9},{2,10},{3,11},{4,12},{5,13},{6,14},{7,15}} | collective-permute-start | bytes 2752520 | tf_op jit(solution)/shard_map/hidden_grad/ppermute | solution.py:172
  158.4 34.9 %collective-permute-start.17 = (bf16[1792,256]{1,0:T(8,128)(2,1)}, bf16[1792,256]{1,0:T(8,128)(2,1)S(1)}, u32[]{:S(2)}, u32[]{:S(2)}) collective-permute-start(bf16[1792,256]{1,0:T(8,128)(2,1)} %get-tuple-element.141), channel_id=1, source_target_pairs={{16,8},{24,16},{17,9},{25,17},{18,10},{26,18},{19,11},{27,19},{20,... | collective-permute-start | bytes 2752520 | tf_op jit(solution)/shard_map/forward/ppermute | solution.py:173
  159.2 34.2 %collective-permute-start.16 = (bf16[1792,256]{1,0:T(8,128)(2,1)}, bf16[1792,256]{1,0:T(8,128)(2,1)}, u32[]{:S(2)}, u32[]{:S(2)}) collective-permute-start(bf16[1792,256]{1,0:T(8,128)(2,1)} %get-tuple-element.142), channel_id=1, source_target_pairs={{0,8},{8,16},{1,9},{9,17},{2,10},{10,18},{3,11},{11,19},{4,12},{12... | collective-permute-start | bytes 2752520 | tf_op jit(solution)/shard_map/forward/ppermute | solution.py:172
  202.5 24.9 %collective-permute-start.20 = (bf16[1792,256]{1,0:T(8,128)(2,1)}, bf16[1792,256]{1,0:T(8,128)(2,1)S(1)}, u32[]{:S(2)}, u32[]{:S(2)}) collective-permute-start(bf16[1792,256]{1,0:T(8,128)(2,1)} %get-tuple-element.139), channel_id=1, source_target_pairs={{8,0},{16,8},{24,16},{9,1},{17,9},{25,17},{10,2},{18,10},{26,18},{... | collective-permute-start | bytes 2752520 | tf_op jit(solution)/shard_map/forward/ppermute | solution.py:173
  203.8 24.9 %collective-permute-start.19 = (bf16[1792,256]{1,0:T(8,128)(2,1)}, bf16[1792,256]{1,0:T(8,128)(2,1)}, u32[]{:S(2)}, u32[]{:S(2)}) collective-permute-start(bf16[1792,256]{1,0:T(8,128)(2,1)} %get-tuple-element.140), channel_id=1, source_target_pairs={{0,8},{8,16},{16,24},{1,9},{9,17},{17,25},{2,10},{10,18},{18,26},{... | collective-permute-start | bytes 2752520 | tf_op jit(solution)/shard_map/forward/ppermute | solution.py:172
  230.3 136.5 %reduce-scatter.2.cloned.1.call-start = ((), (), s32[]{:S(2)}) async-start(), calls=%async_computation.5 | async-start | bytes 4128768 | tf_op jit(solution)/shard_map/layer_out/reduce_scatter | solution.py:355
  236.8 22.0 %collective-permute-start.25 = (bf16[448,1024]{1,0:T(8,128)(2,1)S(1)}, bf16[448,1024]{1,0:T(8,128)(2,1)S(1)}, u32[]{:S(2)}, u32[]{:S(2)}) collective-permute-start(bf16[448,1024]{1,0:T(8,128)(2,1)S(1)} %convolution_convert_fusion.4), channel_id=1, source_target_pairs={{0,4},{1,5},{2,6},{3,7},{4,0},{5,1},{6,2},{7,3},{8,12},{9,13},{10,... | collective-permute-start | bytes 2752520 | tf_op jit(solution)/shard_map/input_grad/ppermute | solution.py:236
  239.7 21.9 %collective-permute-start.23 = (bf16[448,1024]{1,0:T(8,128)(2,1)S(1)}, bf16[448,1024]{1,0:T(8,128)(2,1)S(1)}, u32[]{:S(2)}, u32[]{:S(2)}) collective-permute-start(bf16[448,1024]{1,0:T(8,128)(2,1)S(1)} %convolution_convert_fusion.5), channel_id=1, source_target_pairs={{0,2},{1,3},{2,0},{3,1},{4,6},{5,7},{6,4},{7,5},{8,10},{9,11},{10,... | collective-permute-start | bytes 2752520 | tf_op jit(solution)/shard_map/input_grad/ppermute | solution.py:236
  240.7 22.2 %collective-permute-start.27 = (bf16[896,512]{1,0:T(8,128)(2,1)S(1)}, bf16[896,512]{1,0:T(8,128)(2,1)S(1)}, u32[]{:S(2)}, u32[]{:S(2)}) collective-permute-start(bf16[896,512]{1,0:T(8,128)(2,1)S(1)} %fusion.5), channel_id=1, source_target_pairs={{0,1},{1,0},{2,3},{3,2},{4,5},{5,4},{6,7},{7,6},{8,9},{9,8},{10,11... | collective-permute-start | bytes 2752520 | tf_op jit(solution)/shard_map/input_grad/ppermute | solution.py:327
  274.6 20.0 %collective-permute-start.28 = (bf16[448,1024]{1,0:T(8,128)(2,1)S(1)}, bf16[448,1024]{1,0:T(8,128)(2,1)S(1)}, u32[]{:S(2)}, u32[]{:S(2)}) collective-permute-start(bf16[448,1024]{1,0:T(8,128)(2,1)S(1)} %convolution_convert_fusion.3), channel_id=1, source_target_pairs={{0,2},{1,3},{2,0},{3,1},{4,6},{5,7},{6,4},{7,5},{8,10},{9,11},{10,... | collective-permute-start | bytes 2752520 | tf_op jit(solution)/shard_map/input_grad/ppermute | solution.py:236
  276.4 19.8 %collective-permute-start.29 = (bf16[448,1024]{1,0:T(8,128)(2,1)S(1)}, bf16[448,1024]{1,0:T(8,128)(2,1)S(1)}, u32[]{:S(2)}, u32[]{:S(2)}) collective-permute-start(bf16[448,1024]{1,0:T(8,128)(2,1)S(1)} %convolution_convert_fusion.2), channel_id=1, source_target_pairs={{0,4},{1,5},{2,6},{3,7},{4,0},{5,1},{6,2},{7,3},{8,12},{9,13},{10,... | collective-permute-start | bytes 2752520 | tf_op jit(solution)/shard_map/input_grad/ppermute | solution.py:236
  317.8 24.3 %collective-permute-start.34 = (bf16[224,1024]{1,0:T(8,128)(2,1)S(1)}, bf16[224,1024]{1,0:T(8,128)(2,1)S(1)}, u32[]{:S(2)}, u32[]{:S(2)}) collective-permute-start(bf16[224,1024]{1,0:T(8,128)(2,1)S(1)} %fusion.13), channel_id=1, source_target_pairs={{0,2},{1,3},{2,0},{3,1},{4,6},{5,7},{6,4},{7,5},{8,10},{9,11},{10,... | collective-permute-start | bytes 1376264 | tf_op jit(solution)/shard_map/input_grad/ppermute | solution.py:236
  320.3 21.9 %collective-permute-start.33 = (bf16[224,1024]{1,0:T(8,128)(2,1)S(1)}, bf16[224,1024]{1,0:T(8,128)(2,1)S(1)}, u32[]{:S(2)}, u32[]{:S(2)}) collective-permute-start(bf16[224,1024]{1,0:T(8,128)(2,1)S(1)} %fusion.12), channel_id=1, source_target_pairs={{0,4},{1,5},{2,6},{3,7},{4,0},{5,1},{6,2},{7,3},{8,12},{9,13},{10,... | collective-permute-start | bytes 1376264 | tf_op jit(solution)/shard_map/input_grad/ppermute | solution.py:236
  322.2 19.9 %collective-permute-start.31 = (bf16[56,2048]{1,0:T(8,128)(2,1)S(1)}, bf16[56,2048]{1,0:T(8,128)(2,1)S(1)}, u32[]{:S(2)}, u32[]{:S(2)}) collective-permute-start(bf16[56,2048]{1,0:T(8,128)(2,1)S(1)} %get-tuple-element.149), channel_id=1, source_target_pairs={{0,16},{8,24},{16,0},{24,8},{1,17},{9,25},{17,1},{25,9},{2,18},{10... | collective-permute-start | bytes 688136 | tf_op jit(solution)/shard_map/input_grad/ppermute | solution.py:156
  (51 other events, 509.9 us)
Sparse Core Ops, SparseCore 0:
  11.0 70.5 all-gather.3
  103.2 79.4 all-gather.5
  230.4 73.0 all-gather.7
  312.2 46.9 reduce-scatter.1

commit v4 on v2

--- a/solution.py
+++ b/solution.py
@@ -337,10 +337,11 @@
             arrived = first.send(arrived)
         arrived, both[1] = after((arrived, both[1]))
         second = layer_scatter(both[1], both_weight, chips)
-        waiting, hidden_all = after((next(second), hidden_all))
+        part = finish(first, arrived)
+        waiting, hidden_all, part = after((next(second), hidden_all, part))
         for _ in range(steps - 1):
             waiting = second.send(waiting)
-        first = over_layers(finish(first, arrived))
+        first = over_layers(part)
         arrived, waiting = after((next(first), waiting))
         second = over_layers(finish(second, waiting))
         totals = [finish(first, arrived).astype(BF16), finish(second, next(second)).astype(BF16)]

time: 393 us -> 395 us (level)
    unnamed x66 -> x60, local copies, waits for them, and re-layouts: 15.3 us -> 13.9 us
where the time goes in v4:
time: 395 us; the launch traced here: 394 us
  waiting for transfers between devices  221 us (56%)
  starting transfers between devices  58.7 us (15%)
  matrix products  41.1 us (10%)
  local copies, waits for them, and re-layouts  27 us (7%)
  other arithmetic  22.7 us (6%)
  between operations  14.6 us (4%)
  Pallas kernels  8.91 us (2%)
    ppermute x12, waiting for transfers between devices, across(): lax.ppermute(piece, 'fsdp', [(i, i ^ p) for i in range(n)])  65.2 us
    ppermute x8, waiting for transfers between devices, layer_scatter(): lax.ppermute(part.astype(BF16), 'seq', [(i, i ^ 2 << bit) for i in range(...  46.2 us
    ppermute x3, waiting for transfers between devices, line_steps(): up = lax.ppermute(ahead.astype(BF16), axis, [(i, i + 1) for i in range(k)])  34.7 us
    ppermute x7, waiting for transfers between devices, seq_gather(): lax.ppermute(x, 'seq', [(i, i ^ d) for i in range(n)])  33.7 us
    ppermute x12, starting transfers between devices, across(): lax.ppermute(piece, 'fsdp', [(i, i ^ p) for i in range(n)])  22.6 us
    dot_general x3, matrix products, dot(): return jnp.dot(left, right, preferred_element_type=F32)  21.2 us
    dot_general x13, matrix products, dot_t(): lax.dot_general(left, right, (((1,), (1,)), ((), ())), preferred_element_...  19.9 us
    all_gather x1, waiting for transfers between devices, local(): lax.all_gather(token_rows, 'seq', axis=0, tiled=True, axis_index_groups=s...  17.3 us
  transfers between devices with their start and end apart: 44, of which 26 were waited for; matrix products, arithmetic and copies ran while one was open for 15% of the time, Pallas kernels for 2%

profile of v4, /device:TPU:0, one launch (start us, length us, event | category | flops | bytes accessed | tf_op | source)
XLA Modules:
  0.0 393.8 jit_solution(7475023776556871690)
XLA Ops:
  16.7 7.5 %pick.1 = (bf16[1024,512]{1,0:T(8,128)(2,1)}, bf16[1024,512]{1,0:T(8,128)(2,1)}, bf16[1024,512]{1,0:T(8,128)(2,1)}, bf16[1024,512]{1,0:T(8,128)(2,1)}, bf16[1024,1024]{1,0:T(8,128)(2,1)}, /*index=5*/s32[8,8]{1,0:T(8,128)}) custom-call(s32[1]{0:T(128)} %bitcast.5.layer_ref, s32[8,14]{1,0:T(8,128)} %keep_ref.1, bf16[1024,1792]{1,0:T(8,128)(2,1)} %gate.1, ...), custom_call_target="tpu_custom_call" | custom-call | bytes 12582912 | tf_op jit(solution)/shard_map/pick/pallas_call | solution.py:122
  24.4 15.1 %collective-permute-done.2 = bf16[64,1024]{1,0:T(8,128)(2,1)S(1)} collective-permute-done((bf16[64,1024]{1,0:T(8,128)(2,1)S(1)}, bf16[64,1024]{1,0:T(8,128)(2,1)S(1)}, u32[]{:S(2)}, u32[]{:S(2)}) %collective-permute-start.2) | collective-permute-done | bytes 131104 | tf_op jit(solution)/shard_map/grad_rows/ppermute | solution.py:156
  55.0 8.3 %collective-permute-done.9.refs_3_ = bf16[224,1024]{1,0:T(8,128)(2,1)S(1)} collective-permute-done((bf16[224,1024]{1,0:T(8,128)(2,1)S(1)}, bf16[224,1024]{1,0:T(8,128)(2,1)S(1)}, u32[]{:S(2)}, u32[]{:S(2)}) %collective-permute-start.9) | collective-permute-done | bytes 458784 | tf_op jit(solution)/shard_map/grad_rows/ppermute | solution.py:220
  63.8 9.3 %collective-permute-done.8.refs_6_ = bf16[224,1024]{1,0:T(8,128)(2,1)S(1)} collective-permute-done((bf16[224,1024]{1,0:T(8,128)(2,1)S(1)}, bf16[224,1024]{1,0:T(8,128)(2,1)S(1)}, u32[]{:S(2)}, u32[]{:S(2)}) %collective-permute-start.8) | collective-permute-done | bytes 458784 | tf_op jit(solution)/shard_map/grad_rows/ppermute | solution.py:220
  73.7 9.2 %collective-permute-done.7.refs_2_ = bf16[224,1024]{1,0:T(8,128)(2,1)S(1)} collective-permute-done((bf16[224,1024]{1,0:T(8,128)(2,1)S(1)}, bf16[224,1024]{1,0:T(8,128)(2,1)S(1)}, u32[]{:S(2)}, u32[]{:S(2)}) %collective-permute-start.7) | collective-permute-done | bytes 458784 | tf_op jit(solution)/shard_map/grad_rows/ppermute | solution.py:220
  86.7 12.8 %collective-permute-done.11 = bf16[1024,512]{1,0:T(8,128)(2,1)S(1)} collective-permute-done((bf16[1024,512]{1,0:T(8,128)(2,1)S(1)}, bf16[1024,512]{1,0:T(8,128)(2,1)S(1)}, u32[]{:S(2)}, u32[]{:S(2)}) %collective-permute-start.11) | collective-permute-done | bytes 1048608 | tf_op jit(solution)/shard_map/grad_rows/ppermute | solution.py:156
  115.1 33.4 %collective-permute-done.13 = bf16[1792,256]{1,0:T(8,128)(2,1)S(1)} collective-permute-done((bf16[1792,256]{1,0:T(8,128)(2,1)S(1)}, bf16[1792,256]{1,0:T(8,128)(2,1)S(1)}, u32[]{:S(2)}, u32[]{:S(2)}) %collective-permute-start.13) | collective-permute-done | bytes 917536 | tf_op jit(solution)/shard_map/hidden_grad/ppermute | solution.py:172
  154.1 4.7 %add_convert_fusion.2 = (bf16[1792,256]{1,0:T(8,128)(2,1)}, bf16[1792,256]{1,0:T(8,128)(2,1)}) fusion(bf16[1792,256]{1,0:T(8,128)(2,1)S(1)} %collective-permute-done.14, f32[1792,1024]{1,0:T(8,128)} %copy-done.6, s32[]{:T(128)S(6)} %select_n.133, bf16[1792,256]{1,0:T(8,128)(2,1)} %copy-done.21, s32[]{:T(128)S(6)} %select_n.130), kind=kLoop, calls=%fused_computation.32 | loop fusion | flops 2752512 | bytes 7340040 | tf_op jit(solution)/shard_map/forward/convert_element_type | solution.py:173
  159.5 5.9 %collective-permute-start.16 = (bf16[1792,256]{1,0:T(8,128)(2,1)}, bf16[1792,256]{1,0:T(8,128)(2,1)}, u32[]{:S(2)}, u32[]{:S(2)}) collective-permute-start(bf16[1792,256]{1,0:T(8,128)(2,1)} %get-tuple-element.134), channel_id=1, source_target_pairs={{0,8},{8,16},{1,9},{9,17},{2,10},{10,18},{3,11},{11,19},{4,12},{12... | collective-permute-start | bytes 2752520 | tf_op jit(solution)/shard_map/forward/ppermute | solution.py:172
  165.4 17.3 %all-gather.6.cloned.1.call-done = bf16[1792,2048]{1,0:T(8,128)(2,1)} async-done(((bf16[448,2048]{1,0:T(8,128)(2,1)}), bf16[1792,2048]{1,0:T(8,128)(2,1)}) %all-gather.6.cloned.1.call-update) | async-done | bytes 7340048 | tf_op jit(solution)/shard_map/token_rows/all_gather | solution.py:283
  182.7 10.6 %fusion = f32[1792,1024]{1,0:T(8,128)S(1)} fusion(bf16[1792,2048]{1,0:T(8,128)(2,1)} %all-gather.6.cloned.1.call-done, bf16[2048,512]{1,0:T(8,128)(2,1)} %collective-permute-done.18, bf16[2048,512]{1,0:T(8,128)(2,1)S(1)} %get-tuple-element.140), kind=kOutput, calls=%fused_computation.5 | convolution fusion | flops 7524581376 | bytes 18874368 | tf_op jit(solution)/shard_map/forward/dot_general | solution.py:18
  199.0 4.2 %add_convert_fusion = (bf16[1792,256]{1,0:T(8,128)(2,1)}, bf16[1792,256]{1,0:T(8,128)(2,1)}) fusion(bf16[1792,256]{1,0:T(8,128)(2,1)S(1)} %collective-permute-done.17, f32[1792,1024]{1,0:T(8,128)} %copy-done.6, s32[]{:T(128)S(6)} %select_n.134, bf16[1792,256]{1,0:T(8,128)(2,1)} %collective-permute-done.16, s32[]{:T(128)S(6)} %select_n.129), kind=kLoop, calls=%fused_computation.30 | loop fusion | flops 2752512 | bytes 7340040 | tf_op jit(solution)/shard_map/forward/convert_element_type | solution.py:173
  204.6 5.5 %collective-permute-start.19 = (bf16[1792,256]{1,0:T(8,128)(2,1)}, bf16[1792,256]{1,0:T(8,128)(2,1)}, u32[]{:S(2)}, u32[]{:S(2)}) collective-permute-start(bf16[1792,256]{1,0:T(8,128)(2,1)} %get-tuple-element.132), channel_id=1, source_target_pairs={{0,8},{8,16},{16,24},{1,9},{9,17},{17,25},{2,10},{10,18},{18,26},{... | collective-permute-start | bytes 2752520 | tf_op jit(solution)/shard_map/forward/ppermute | solution.py:172
  221.4 6.7 %collective-permute-done.20 = bf16[1792,256]{1,0:T(8,128)(2,1)S(1)} collective-permute-done((bf16[1792,256]{1,0:T(8,128)(2,1)}, bf16[1792,256]{1,0:T(8,128)(2,1)S(1)}, u32[]{:S(2)}, u32[]{:S(2)}) %collective-permute-start.20) | collective-permute-done | bytes 917536 | tf_op jit(solution)/shard_map/forward/ppermute | solution.py:173
  245.4 17.2 %collective-permute-done.25 = bf16[448,1024]{1,0:T(8,128)(2,1)S(1)} collective-permute-done((bf16[448,1024]{1,0:T(8,128)(2,1)S(1)}, bf16[448,1024]{1,0:T(8,128)(2,1)S(1)}, u32[]{:S(2)}, u32[]{:S(2)}) %collective-permute-start.25) | collective-permute-done | bytes 917536 | tf_op jit(solution)/shard_map/input_grad/ppermute | solution.py:236
  269.3 7.0 %collective-permute-done.26 = bf16[224,1024]{1,0:T(8,128)(2,1)S(1)} collective-permute-done((bf16[224,1024]{1,0:T(8,128)(2,1)S(1)}, bf16[224,1024]{1,0:T(8,128)(2,1)S(1)}, u32[]{:S(2)}, u32[]{:S(2)}) %collective-permute-start.26) | collective-permute-done | bytes 458784 | tf_op jit(solution)/shard_map/input_grad/ppermute | solution.py:236
  288.2 14.0 %collective-permute-done.28 = bf16[448,1024]{1,0:T(8,128)(2,1)S(1)} collective-permute-done((bf16[448,1024]{1,0:T(8,128)(2,1)S(1)}, bf16[448,1024]{1,0:T(8,128)(2,1)S(1)}, u32[]{:S(2)}, u32[]{:S(2)}) %collective-permute-start.28) | collective-permute-done | bytes 917536 | tf_op jit(solution)/shard_map/input_grad/ppermute | solution.py:236
  308.0 8.6 %convolution_convert_fusion = bf16[1792,1024]{1,0:T(8,128)(2,1)} fusion(bf16[1792,1024]{1,0:T(8,128)(2,1)} %all-gather.8.cloned.1.call-done, bf16[1024,1024]{1,0:T(8,128)(2,1)} %get-tuple-element.87), kind=kOutput, calls=%fused_computation.6 | convolution fusion | flops 3759931392 | bytes 9437184 | tf_op jit(solution)/shard_map/layer_out/dot_general | solution.py:18
  328.0 6.0 %collective-permute-done.32 = bf16[56,2048]{1,0:T(8,128)(2,1)S(1)} collective-permute-done((bf16[56,2048]{1,0:T(8,128)(2,1)S(1)}, bf16[56,2048]{1,0:T(8,128)(2,1)S(1)}, u32[]{:S(2)}, u32[]{:S(2)}) %collective-permute-start.32) | collective-permute-done | bytes 229408 | tf_op jit(solution)/shard_map/input_grad/ppermute | solution.py:156
  334.1 10.0 %collective-permute-done.31 = bf16[56,2048]{1,0:T(8,128)(2,1)S(1)} collective-permute-done((bf16[56,2048]{1,0:T(8,128)(2,1)S(1)}, bf16[56,2048]{1,0:T(8,128)(2,1)S(1)}, u32[]{:S(2)}, u32[]{:S(2)}) %collective-permute-start.31) | collective-permute-done | bytes 229408 | tf_op jit(solution)/shard_map/input_grad/ppermute | solution.py:156
  349.5 5.1 %collective-permute-done.35 = bf16[56,2048]{1,0:T(8,128)(2,1)S(1)} collective-permute-done((bf16[56,2048]{1,0:T(8,128)(2,1)S(1)}, bf16[56,2048]{1,0:T(8,128)(2,1)S(1)}, u32[]{:S(2)}, u32[]{:S(2)}) %collective-permute-start.35) | collective-permute-done | bytes 229408 | tf_op jit(solution)/shard_map/input_grad/ppermute | solution.py:156
  354.6 5.6 %collective-permute-done.37 = bf16[56,2048]{1,0:T(8,128)(2,1)S(1)} collective-permute-done((bf16[56,2048]{1,0:T(8,128)(2,1)S(1)}, bf16[56,2048]{1,0:T(8,128)(2,1)S(1)}, u32[]{:S(2)}, u32[]{:S(2)}) %collective-permute-start.37) | collective-permute-done | bytes 229408 | tf_op jit(solution)/shard_map/input_grad/ppermute | solution.py:156
  360.2 8.2 %collective-permute-done.36 = bf16[56,2048]{1,0:T(8,128)(2,1)S(1)} collective-permute-done((bf16[56,2048]{1,0:T(8,128)(2,1)S(1)}, bf16[56,2048]{1,0:T(8,128)(2,1)S(1)}, u32[]{:S(2)}, u32[]{:S(2)}) %collective-permute-start.36) | collective-permute-done | bytes 229408 | tf_op jit(solution)/shard_map/input_grad/ppermute | solution.py:156
  373.6 12.8 %all-to-all-done = bf16[4,56,1024]{2,1,0:T(8,128)(2,1)S(1)} async-done(((bf16[4,56,1024]{2,1,0:T(8,128)(2,1)}), bf16[4,56,1024]{2,1,0:T(8,128)(2,1)S(1)}, u32[]{:S(2)}, u32[]{:S(2)}) %all-to-all-start) | async-done | bytes 458784 | tf_op jit(solution)/shard_map/layer_out/all_to_all | solution.py:357
  (203 shorter events, 134.1 us)
Async XLA Ops:
  7.2 95.8 %all-gather.4.cloned.1.call-start = ((), (), s32[]{:S(2)}) async-start(), calls=%async_computation.2 | async-start | bytes 2293760 | tf_op jit(solution)/shard_map/token_rows/all_gather | solution.py:280
  10.9 171.8 %all-gather.6.cloned.1.call-start = ((), (), s32[]{:S(2)}) async-start(), calls=%async_computation.3 | async-start | bytes 9175040 | tf_op jit(solution)/shard_map/token_rows/all_gather | solution.py:283
  14.1 25.4 %collective-permute-start.3 = (bf16[64,1024]{1,0:T(8,128)(2,1)S(1)}, bf16[64,1024]{1,0:T(8,128)(2,1)S(1)}, u32[]{:S(2)}, u32[]{:S(2)}) collective-permute-start(bf16[64,1024]{1,0:T(8,128)(2,1)S(1)} %get-tuple-element.170), channel_id=1, source_target_pairs={{0,24},{8,16},{16,8},{24,0},{1,25},{9,17},{17,9},{25,1},{2,26},{10... | collective-permute-start | bytes 393224 | tf_op jit(solution)/shard_map/grad_rows/ppermute | solution.py:156
  16.6 22.9 %collective-permute-start.2 = (bf16[64,1024]{1,0:T(8,128)(2,1)S(1)}, bf16[64,1024]{1,0:T(8,128)(2,1)S(1)}, u32[]{:S(2)}, u32[]{:S(2)}) collective-permute-start(bf16[64,1024]{1,0:T(8,128)(2,1)S(1)} %get-tuple-element.172), channel_id=1, source_target_pairs={{0,16},{8,24},{16,0},{24,8},{1,17},{9,25},{17,1},{25,9},{2,18},{10... | collective-permute-start | bytes 393224 | tf_op jit(solution)/shard_map/grad_rows/ppermute | solution.py:156
  39.7 59.9 %collective-permute-start.11 = (bf16[1024,512]{1,0:T(8,128)(2,1)S(1)}, bf16[1024,512]{1,0:T(8,128)(2,1)S(1)}, u32[]{:S(2)}, u32[]{:S(2)}) collective-permute-start(bf16[1024,512]{1,0:T(8,128)(2,1)S(1)} %copy-done.27), channel_id=1, source_target_pairs={{0,8},{8,0},{16,24},{24,16},{1,9},{9,1},{17,25},{25,17},{2,10},{10... | collective-permute-start | bytes 3145736 | tf_op jit(solution)/shard_map/grad_rows/ppermute | solution.py:156
  42.5 60.5 %collective-permute-start.12 = (bf16[1024,512]{1,0:T(8,128)(2,1)S(1)}, bf16[1024,512]{1,0:T(8,128)(2,1)}, u32[]{:S(2)}, u32[]{:S(2)}) collective-permute-start(bf16[1024,512]{1,0:T(8,128)(2,1)S(1)} %copy-done.26), channel_id=1, source_target_pairs={{0,16},{8,24},{16,0},{24,8},{1,17},{9,25},{17,1},{25,9},{2,18},{10... | collective-permute-start | bytes 3145736 | tf_op jit(solution)/shard_map/grad_rows/ppermute | solution.py:156
  48.4 24.6 %collective-permute-start.8 = (bf16[224,1024]{1,0:T(8,128)(2,1)S(1)}, bf16[224,1024]{1,0:T(8,128)(2,1)S(1)}, u32[]{:S(2)}, u32[]{:S(2)}) collective-permute-start(bf16[224,1024]{1,0:T(8,128)(2,1)S(1)} %bitcast.103), channel_id=1, source_target_pairs={{0,5},{1,4},{2,7},{3,6},{4,1},{5,0},{6,3},{7,2},{8,13},{9,12},{10,... | collective-permute-start | bytes 1376264 | tf_op jit(solution)/shard_map/grad_rows/ppermute | solution.py:220
  53.2 29.6 %collective-permute-start.7 = (bf16[224,1024]{1,0:T(8,128)(2,1)S(1)}, bf16[224,1024]{1,0:T(8,128)(2,1)S(1)}, u32[]{:S(2)}, u32[]{:S(2)}) collective-permute-start(bf16[224,1024]{1,0:T(8,128)(2,1)S(1)} %bitcast.104), channel_id=1, source_target_pairs={{0,4},{1,5},{2,6},{3,7},{4,0},{5,1},{6,2},{7,3},{8,12},{9,13},{10,... | collective-permute-start | bytes 1376264 | tf_op jit(solution)/shard_map/grad_rows/ppermute | solution.py:220
  103.0 204.9 %all-gather.8.cloned.1.call-start = ((), (), s32[]{:S(2)}) async-start(), calls=%async_computation.4 | async-start | bytes 4587520 | tf_op jit(solution)/shard_map/forward/all_gather | solution.py:311
  103.1 46.3 %collective-permute-start.15 = (bf16[1024,512]{1,0:T(8,128)(2,1)}, bf16[1024,512]{1,0:T(8,128)(2,1)S(1)}, u32[]{:S(2)}, u32[]{:S(2)}) collective-permute-start(bf16[1024,512]{1,0:T(8,128)(2,1)} %get-tuple-element.91), channel_id=1, source_target_pairs={{0,24},{8,16},{16,8},{24,0},{1,25},{9,17},{17,9},{25,1},{2,26},{10... | collective-permute-start | bytes 3145736 | tf_op jit(solution)/shard_map/hidden_grad/ppermute | solution.py:156
  113.4 35.0 %collective-permute-start.13 = (bf16[1792,256]{1,0:T(8,128)(2,1)S(1)}, bf16[1792,256]{1,0:T(8,128)(2,1)S(1)}, u32[]{:S(2)}, u32[]{:S(2)}) collective-permute-start(bf16[1792,256]{1,0:T(8,128)(2,1)S(1)} %get-tuple-element.136), channel_id=1, source_target_pairs={{0,8},{1,9},{2,10},{3,11},{4,12},{5,13},{6,14},{7,15}} | collective-permute-start | bytes 2752520 | tf_op jit(solution)/shard_map/hidden_grad/ppermute | solution.py:172
  158.8 34.5 %collective-permute-start.17 = (bf16[1792,256]{1,0:T(8,128)(2,1)}, bf16[1792,256]{1,0:T(8,128)(2,1)S(1)}, u32[]{:S(2)}, u32[]{:S(2)}) collective-permute-start(bf16[1792,256]{1,0:T(8,128)(2,1)} %get-tuple-element.133), channel_id=1, source_target_pairs={{16,8},{24,16},{17,9},{25,17},{18,10},{26,18},{19,11},{27,19},{20,... | collective-permute-start | bytes 2752520 | tf_op jit(solution)/shard_map/forward/ppermute | solution.py:173
  159.5 33.8 %collective-permute-start.16 = (bf16[1792,256]{1,0:T(8,128)(2,1)}, bf16[1792,256]{1,0:T(8,128)(2,1)}, u32[]{:S(2)}, u32[]{:S(2)}) collective-permute-start(bf16[1792,256]{1,0:T(8,128)(2,1)} %get-tuple-element.134), channel_id=1, source_target_pairs={{0,8},{8,16},{1,9},{9,17},{2,10},{10,18},{3,11},{11,19},{4,12},{12... | collective-permute-start | bytes 2752520 | tf_op jit(solution)/shard_map/forward/ppermute | solution.py:172
  203.3 24.9 %collective-permute-start.20 = (bf16[1792,256]{1,0:T(8,128)(2,1)}, bf16[1792,256]{1,0:T(8,128)(2,1)S(1)}, u32[]{:S(2)}, u32[]{:S(2)}) collective-permute-start(bf16[1792,256]{1,0:T(8,128)(2,1)} %get-tuple-element.131), channel_id=1, source_target_pairs={{8,0},{16,8},{24,16},{9,1},{17,9},{25,17},{10,2},{18,10},{26,18},{... | collective-permute-start | bytes 2752520 | tf_op jit(solution)/shard_map/forward/ppermute | solution.py:173
  204.6 24.9 %collective-permute-start.19 = (bf16[1792,256]{1,0:T(8,128)(2,1)}, bf16[1792,256]{1,0:T(8,128)(2,1)}, u32[]{:S(2)}, u32[]{:S(2)}) collective-permute-start(bf16[1792,256]{1,0:T(8,128)(2,1)} %get-tuple-element.132), channel_id=1, source_target_pairs={{0,8},{8,16},{16,24},{1,9},{9,17},{17,25},{2,10},{10,18},{18,26},{... | collective-permute-start | bytes 2752520 | tf_op jit(solution)/shard_map/forward/ppermute | solution.py:172
  234.6 134.2 %reduce-scatter.2.cloned.1.call-start = ((), (), s32[]{:S(2)}) async-start(), calls=%async_computation.5 | async-start | bytes 4128768 | tf_op jit(solution)/shard_map/layer_out/reduce_scatter | solution.py:356
  239.8 22.8 %collective-permute-start.25 = (bf16[448,1024]{1,0:T(8,128)(2,1)S(1)}, bf16[448,1024]{1,0:T(8,128)(2,1)S(1)}, u32[]{:S(2)}, u32[]{:S(2)}) collective-permute-start(bf16[448,1024]{1,0:T(8,128)(2,1)S(1)} %convolution_convert_fusion.3), channel_id=1, source_target_pairs={{0,4},{1,5},{2,6},{3,7},{4,0},{5,1},{6,2},{7,3},{8,12},{9,13},{10,... | collective-permute-start | bytes 2752520 | tf_op jit(solution)/shard_map/input_grad/ppermute | solution.py:236
  243.9 23.0 %collective-permute-start.23 = (bf16[448,1024]{1,0:T(8,128)(2,1)S(1)}, bf16[448,1024]{1,0:T(8,128)(2,1)S(1)}, u32[]{:S(2)}, u32[]{:S(2)}) collective-permute-start(bf16[448,1024]{1,0:T(8,128)(2,1)S(1)} %convolution_convert_fusion.4), channel_id=1, source_target_pairs={{0,2},{1,3},{2,0},{3,1},{4,6},{5,7},{6,4},{7,5},{8,10},{9,11},{10,... | collective-permute-start | bytes 2752520 | tf_op jit(solution)/shard_map/input_grad/ppermute | solution.py:236
  245.1 23.9 %collective-permute-start.27 = (bf16[896,512]{1,0:T(8,128)(2,1)S(1)}, bf16[896,512]{1,0:T(8,128)(2,1)S(1)}, u32[]{:S(2)}, u32[]{:S(2)}) collective-permute-start(bf16[896,512]{1,0:T(8,128)(2,1)S(1)} %fusion.5), channel_id=1, source_target_pairs={{0,1},{1,0},{2,3},{3,2},{4,5},{5,4},{6,7},{7,6},{8,9},{9,8},{10,11... | collective-permute-start | bytes 2752520 | tf_op jit(solution)/shard_map/input_grad/ppermute | solution.py:327
  281.6 20.5 %collective-permute-start.28 = (bf16[448,1024]{1,0:T(8,128)(2,1)S(1)}, bf16[448,1024]{1,0:T(8,128)(2,1)S(1)}, u32[]{:S(2)}, u32[]{:S(2)}) collective-permute-start(bf16[448,1024]{1,0:T(8,128)(2,1)S(1)} %convolution_convert_fusion.2), channel_id=1, source_target_pairs={{0,2},{1,3},{2,0},{3,1},{4,6},{5,7},{6,4},{7,5},{8,10},{9,11},{10,... | collective-permute-start | bytes 2752520 | tf_op jit(solution)/shard_map/input_grad/ppermute | solution.py:236
  283.4 20.7 %collective-permute-start.29 = (bf16[448,1024]{1,0:T(8,128)(2,1)S(1)}, bf16[448,1024]{1,0:T(8,128)(2,1)S(1)}, u32[]{:S(2)}, u32[]{:S(2)}) collective-permute-start(bf16[448,1024]{1,0:T(8,128)(2,1)S(1)} %convolution_convert_fusion.1), channel_id=1, source_target_pairs={{0,4},{1,5},{2,6},{3,7},{4,0},{5,1},{6,2},{7,3},{8,12},{9,13},{10,... | collective-permute-start | bytes 2752520 | tf_op jit(solution)/shard_map/input_grad/ppermute | solution.py:236
  319.6 24.4 %collective-permute-start.34 = (bf16[224,1024]{1,0:T(8,128)(2,1)S(1)}, bf16[224,1024]{1,0:T(8,128)(2,1)S(1)}, u32[]{:S(2)}, u32[]{:S(2)}) collective-permute-start(bf16[224,1024]{1,0:T(8,128)(2,1)S(1)} %fusion.13), channel_id=1, source_target_pairs={{0,2},{1,3},{2,0},{3,1},{4,6},{5,7},{6,4},{7,5},{8,10},{9,11},{10,... | collective-permute-start | bytes 1376264 | tf_op jit(solution)/shard_map/input_grad/ppermute | solution.py:236
  321.9 22.1 %collective-permute-start.33 = (bf16[224,1024]{1,0:T(8,128)(2,1)S(1)}, bf16[224,1024]{1,0:T(8,128)(2,1)S(1)}, u32[]{:S(2)}, u32[]{:S(2)}) collective-permute-start(bf16[224,1024]{1,0:T(8,128)(2,1)S(1)} %fusion.12), channel_id=1, source_target_pairs={{0,4},{1,5},{2,6},{3,7},{4,0},{5,1},{6,2},{7,3},{8,12},{9,13},{10,... | collective-permute-start | bytes 1376264 | tf_op jit(solution)/shard_map/input_grad/ppermute | solution.py:236
  324.1 19.9 %collective-permute-start.31 = (bf16[56,2048]{1,0:T(8,128)(2,1)S(1)}, bf16[56,2048]{1,0:T(8,128)(2,1)S(1)}, u32[]{:S(2)}, u32[]{:S(2)}) collective-permute-start(bf16[56,2048]{1,0:T(8,128)(2,1)S(1)} %get-tuple-element.151), channel_id=1, source_target_pairs={{0,16},{8,24},{16,0},{24,8},{1,17},{9,25},{17,1},{25,9},{2,18},{10... | collective-permute-start | bytes 688136 | tf_op jit(solution)/shard_map/input_grad/ppermute | solution.py:156
  (50 other events, 562.1 us)
Sparse Core Ops, SparseCore 0:
  11.0 70.5 all-gather.3
  103.2 79.4 all-gather.5
  234.7 73.1 all-gather.7
  316.7 46.9 reduce-scatter.1

commit v5 on v2

--- a/solution.py
+++ b/solution.py
@@ -343,7 +343,10 @@
         first = over_layers(finish(first, arrived))
         arrived, waiting = after((next(first), waiting))
         second = over_layers(finish(second, waiting))
-        totals = [finish(first, arrived).astype(BF16), finish(second, next(second)).astype(BF16)]
+        out_part = dot(hidden_all, down_pick).astype(BF16)
+        out = lax.psum_scatter(out_part, "seq", scatter_dimension=0, tiled=True)
+        waiting, out = after((next(second), out))
+        totals = [finish(first, arrived).astype(BF16), finish(second, waiting).astype(BF16)]
         here = jnp.where(core == 0, totals[0], totals[1])
         there = lax.ppermute(jnp.where(core == 0, totals[1], totals[0]), "seq", swap)
         input_grad = jnp.where(
@@ -351,8 +354,6 @@
         )
 
     with jax.named_scope("layer_out"):
-        out_part = dot(hidden_all, down_pick).astype(BF16)
-        out = lax.psum_scatter(out_part, "seq", scatter_dimension=0, tiled=True)
         out = lax.all_to_all(out.reshape(nf, rows, deep), "fsdp", 0, 0, tiled=False)
         layer_out = out.transpose(1, 0, 2).reshape(rows, wide)
     return layer_out, input_grad

time: 393 us -> 393 us (level)
    unnamed x66 -> x80, local copies, waits for them, and re-layouts: 15.3 us -> 16.1 us
  transfers between devices with their start and end apart: 44 -> 44, of which waited for: 26 -> 25; matrix products, arithmetic and copies ran while one was open for 15% -> 15% of each run, Pallas kernels for 2% -> 2%
where the time goes in v5:
time: 393 us; the launch traced here: 392 us
  waiting for transfers between devices  221 us (56%)
  starting transfers between devices  59.6 us (15%)
  matrix products  37.8 us (10%)
  local copies, waits for them, and re-layouts  29.7 us (8%)
  other arithmetic  20.7 us (5%)
  between operations  14.7 us (4%)
  Pallas kernels  8.94 us (2%)
    ppermute x12, waiting for transfers between devices, across(): lax.ppermute(piece, 'fsdp', [(i, i ^ p) for i in range(n)])  62 us
    ppermute x8, waiting for transfers between devices, layer_scatter(): lax.ppermute(part.astype(BF16), 'seq', [(i, i ^ 2 << bit) for i in range(...  44.8 us
    ppermute x3, waiting for transfers between devices, line_steps(): up = lax.ppermute(ahead.astype(BF16), axis, [(i, i + 1) for i in range(k)])  34.7 us
    ppermute x7, waiting for transfers between devices, seq_gather(): lax.ppermute(x, 'seq', [(i, i ^ d) for i in range(n)])  33.7 us
    ppermute x12, starting transfers between devices, across(): lax.ppermute(piece, 'fsdp', [(i, i ^ p) for i in range(n)])  23.5 us
    dot_general x3, matrix products, dot(): return jnp.dot(left, right, preferred_element_type=F32)  21.1 us
    all_gather x1, waiting for transfers between devices, local(): lax.all_gather(token_rows, 'seq', axis=0, tiled=True, axis_index_groups=s...  18 us
    dot_general x13, matrix products, dot_t(): lax.dot_general(left, right, (((1,), (1,)), ((), ())), preferred_element_...  16.7 us
  transfers between devices with their start and end apart: 44, of which 25 were waited for; matrix products, arithmetic and copies ran while one was open for 15% of the time, Pallas kernels for 2%

profile of v5, /device:TPU:0, one launch (start us, length us, event | category | flops | bytes accessed | tf_op | source)
XLA Modules:
  0.0 392.3 jit_solution(11453434876455958350)
XLA Ops:
  16.7 7.5 %pick.1 = (bf16[1024,512]{1,0:T(8,128)(2,1)}, bf16[1024,512]{1,0:T(8,128)(2,1)}, bf16[1024,512]{1,0:T(8,128)(2,1)}, bf16[1024,512]{1,0:T(8,128)(2,1)}, bf16[1024,1024]{1,0:T(8,128)(2,1)}, /*index=5*/s32[8,8]{1,0:T(8,128)}) custom-call(s32[1]{0:T(128)} %bitcast.5.layer_ref, s32[8,14]{1,0:T(8,128)} %keep_ref.1, bf16[1024,1792]{1,0:T(8,128)(2,1)} %gate.1, ...), custom_call_target="tpu_custom_call" | custom-call | bytes 12582912 | tf_op jit(solution)/shard_map/pick/pallas_call | solution.py:122
  24.4 15.1 %collective-permute-done.2 = bf16[64,1024]{1,0:T(8,128)(2,1)S(1)} collective-permute-done((bf16[64,1024]{1,0:T(8,128)(2,1)S(1)}, bf16[64,1024]{1,0:T(8,128)(2,1)S(1)}, u32[]{:S(2)}, u32[]{:S(2)}) %collective-permute-start.2) | collective-permute-done | bytes 131104 | tf_op jit(solution)/shard_map/grad_rows/ppermute | solution.py:156
  55.0 8.3 %collective-permute-done.9.refs_3_ = bf16[224,1024]{1,0:T(8,128)(2,1)S(1)} collective-permute-done((bf16[224,1024]{1,0:T(8,128)(2,1)S(1)}, bf16[224,1024]{1,0:T(8,128)(2,1)S(1)}, u32[]{:S(2)}, u32[]{:S(2)}) %collective-permute-start.9) | collective-permute-done | bytes 458784 | tf_op jit(solution)/shard_map/grad_rows/ppermute | solution.py:220
  63.8 9.3 %collective-permute-done.8.refs_6_ = bf16[224,1024]{1,0:T(8,128)(2,1)S(1)} collective-permute-done((bf16[224,1024]{1,0:T(8,128)(2,1)S(1)}, bf16[224,1024]{1,0:T(8,128)(2,1)S(1)}, u32[]{:S(2)}, u32[]{:S(2)}) %collective-permute-start.8) | collective-permute-done | bytes 458784 | tf_op jit(solution)/shard_map/grad_rows/ppermute | solution.py:220
  73.7 9.2 %collective-permute-done.7.refs_2_ = bf16[224,1024]{1,0:T(8,128)(2,1)S(1)} collective-permute-done((bf16[224,1024]{1,0:T(8,128)(2,1)S(1)}, bf16[224,1024]{1,0:T(8,128)(2,1)S(1)}, u32[]{:S(2)}, u32[]{:S(2)}) %collective-permute-start.7) | collective-permute-done | bytes 458784 | tf_op jit(solution)/shard_map/grad_rows/ppermute | solution.py:220
  86.7 12.8 %collective-permute-done.11 = bf16[1024,512]{1,0:T(8,128)(2,1)S(1)} collective-permute-done((bf16[1024,512]{1,0:T(8,128)(2,1)S(1)}, bf16[1024,512]{1,0:T(8,128)(2,1)S(1)}, u32[]{:S(2)}, u32[]{:S(2)}) %collective-permute-start.11) | collective-permute-done | bytes 1048608 | tf_op jit(solution)/shard_map/grad_rows/ppermute | solution.py:156
  115.1 33.4 %collective-permute-done.13 = bf16[1792,256]{1,0:T(8,128)(2,1)S(1)} collective-permute-done((bf16[1792,256]{1,0:T(8,128)(2,1)S(1)}, bf16[1792,256]{1,0:T(8,128)(2,1)S(1)}, u32[]{:S(2)}, u32[]{:S(2)}) %collective-permute-start.13) | collective-permute-done | bytes 917536 | tf_op jit(solution)/shard_map/hidden_grad/ppermute | solution.py:172
  153.2 4.8 %add_convert_fusion.2 = (bf16[1792,256]{1,0:T(8,128)(2,1)}, bf16[1792,256]{1,0:T(8,128)(2,1)}) fusion(bf16[1792,256]{1,0:T(8,128)(2,1)S(1)} %collective-permute-done.14, f32[1792,1024]{1,0:T(8,128)} %copy-done.6, s32[]{:T(128)S(6)} %select_n.133, bf16[1792,256]{1,0:T(8,128)(2,1)} %copy-done.20, s32[]{:T(128)S(6)} %select_n.130), kind=kLoop, calls=%fused_computation.32 | loop fusion | flops 2752512 | bytes 7340040 | tf_op jit(solution)/shard_map/forward/convert_element_type | solution.py:173
  158.7 6.0 %collective-permute-start.16 = (bf16[1792,256]{1,0:T(8,128)(2,1)}, bf16[1792,256]{1,0:T(8,128)(2,1)}, u32[]{:S(2)}, u32[]{:S(2)}) collective-permute-start(bf16[1792,256]{1,0:T(8,128)(2,1)} %get-tuple-element.140), channel_id=1, source_target_pairs={{0,8},{8,16},{1,9},{9,17},{2,10},{10,18},{3,11},{11,19},{4,12},{12... | collective-permute-start | bytes 2752520 | tf_op jit(solution)/shard_map/forward/ppermute | solution.py:172
  164.7 18.0 %all-gather.6.cloned.1.call-done = bf16[1792,2048]{1,0:T(8,128)(2,1)} async-done(((bf16[448,2048]{1,0:T(8,128)(2,1)}), bf16[1792,2048]{1,0:T(8,128)(2,1)}) %all-gather.6.cloned.1.call-update) | async-done | bytes 7340048 | tf_op jit(solution)/shard_map/token_rows/all_gather | solution.py:283
  182.7 10.6 %fusion = f32[1792,1024]{1,0:T(8,128)S(1)} fusion(bf16[1792,2048]{1,0:T(8,128)(2,1)} %all-gather.6.cloned.1.call-done, bf16[2048,512]{1,0:T(8,128)(2,1)} %collective-permute-done.18, bf16[2048,512]{1,0:T(8,128)(2,1)S(1)} %get-tuple-element.146), kind=kOutput, calls=%fused_computation.5 | convolution fusion | flops 7524581376 | bytes 18874368 | tf_op jit(solution)/shard_map/forward/dot_general | solution.py:18
  199.0 4.2 %add_convert_fusion = (bf16[1792,256]{1,0:T(8,128)(2,1)}, bf16[1792,256]{1,0:T(8,128)(2,1)}) fusion(bf16[1792,256]{1,0:T(8,128)(2,1)S(1)} %collective-permute-done.17, f32[1792,1024]{1,0:T(8,128)} %copy-done.6, s32[]{:T(128)S(6)} %select_n.134, bf16[1792,256]{1,0:T(8,128)(2,1)} %collective-permute-done.16, s32[]{:T(128)S(6)} %select_n.129), kind=kLoop, calls=%fused_computation.30 | loop fusion | flops 2752512 | bytes 7340040 | tf_op jit(solution)/shard_map/forward/convert_element_type | solution.py:173
  204.5 5.6 %collective-permute-start.19 = (bf16[1792,256]{1,0:T(8,128)(2,1)}, bf16[1792,256]{1,0:T(8,128)(2,1)}, u32[]{:S(2)}, u32[]{:S(2)}) collective-permute-start(bf16[1792,256]{1,0:T(8,128)(2,1)} %get-tuple-element.138), channel_id=1, source_target_pairs={{0,8},{8,16},{16,24},{1,9},{9,17},{17,25},{2,10},{10,18},{18,26},{... | collective-permute-start | bytes 2752520 | tf_op jit(solution)/shard_map/forward/ppermute | solution.py:172
  221.3 6.7 %collective-permute-done.20 = bf16[1792,256]{1,0:T(8,128)(2,1)S(1)} collective-permute-done((bf16[1792,256]{1,0:T(8,128)(2,1)}, bf16[1792,256]{1,0:T(8,128)(2,1)S(1)}, u32[]{:S(2)}, u32[]{:S(2)}) %collective-permute-start.20) | collective-permute-done | bytes 917536 | tf_op jit(solution)/shard_map/forward/ppermute | solution.py:173
  241.9 17.9 %collective-permute-done.25 = bf16[448,1024]{1,0:T(8,128)(2,1)S(1)} collective-permute-done((bf16[448,1024]{1,0:T(8,128)(2,1)S(1)}, bf16[448,1024]{1,0:T(8,128)(2,1)S(1)}, u32[]{:S(2)}, u32[]{:S(2)}) %collective-permute-start.25) | collective-permute-done | bytes 917536 | tf_op jit(solution)/shard_map/input_grad/ppermute | solution.py:236
  265.0 7.2 %collective-permute-done.26 = bf16[224,1024]{1,0:T(8,128)(2,1)S(1)} collective-permute-done((bf16[224,1024]{1,0:T(8,128)(2,1)S(1)}, bf16[224,1024]{1,0:T(8,128)(2,1)S(1)}, u32[]{:S(2)}, u32[]{:S(2)}) %collective-permute-start.26) | collective-permute-done | bytes 458784 | tf_op jit(solution)/shard_map/input_grad/ppermute | solution.py:236
  278.6 16.2 %collective-permute-done.31 = bf16[448,1024]{1,0:T(8,128)(2,1)S(1)} collective-permute-done((bf16[448,1024]{1,0:T(8,128)(2,1)S(1)}, bf16[448,1024]{1,0:T(8,128)(2,1)S(1)}, u32[]{:S(2)}, u32[]{:S(2)}) %collective-permute-start.31) | collective-permute-done | bytes 917536 | tf_op jit(solution)/shard_map/input_grad/ppermute | solution.py:236
  297.6 6.6 %all-gather.8.cloned.1.call-done = bf16[1792,1024]{1,0:T(8,128)(2,1)} async-done(((bf16[1792,256]{1,0:T(8,128)(2,1)}), bf16[1792,1024]{1,0:T(8,128)(2,1)}) %all-gather.8.cloned.1.call-update) | async-done | bytes 3670032 | tf_op jit(solution)/shard_map/forward/all_gather | solution.py:311
  304.2 8.5 %convolution_convert_fusion = bf16[1792,1024]{1,0:T(8,128)(2,1)} fusion(bf16[1792,1024]{1,0:T(8,128)(2,1)} %all-gather.8.cloned.1.call-done, bf16[1024,1024]{1,0:T(8,128)(2,1)} %get-tuple-element.90), kind=kOutput, calls=%fused_computation.6 | convolution fusion | flops 3759931392 | bytes 9437184 | tf_op jit(solution)/shard_map/input_grad/dot_general | solution.py:18
  327.2 6.0 %collective-permute-done.30 = bf16[56,2048]{1,0:T(8,128)(2,1)S(1)} collective-permute-done((bf16[56,2048]{1,0:T(8,128)(2,1)S(1)}, bf16[56,2048]{1,0:T(8,128)(2,1)S(1)}, u32[]{:S(2)}, u32[]{:S(2)}) %collective-permute-start.30) | collective-permute-done | bytes 229408 | tf_op jit(solution)/shard_map/input_grad/ppermute | solution.py:156
  333.2 9.7 %collective-permute-done.29 = bf16[56,2048]{1,0:T(8,128)(2,1)S(1)} collective-permute-done((bf16[56,2048]{1,0:T(8,128)(2,1)S(1)}, bf16[56,2048]{1,0:T(8,128)(2,1)S(1)}, u32[]{:S(2)}, u32[]{:S(2)}) %collective-permute-start.29) | collective-permute-done | bytes 229408 | tf_op jit(solution)/shard_map/input_grad/ppermute | solution.py:156
  350.1 6.1 %collective-permute-done.37 = bf16[56,2048]{1,0:T(8,128)(2,1)S(1)} collective-permute-done((bf16[56,2048]{1,0:T(8,128)(2,1)S(1)}, bf16[56,2048]{1,0:T(8,128)(2,1)S(1)}, u32[]{:S(2)}, u32[]{:S(2)}) %collective-permute-start.37) | collective-permute-done | bytes 229408 | tf_op jit(solution)/shard_map/input_grad/ppermute | solution.py:156
  356.2 9.9 %collective-permute-done.36 = bf16[56,2048]{1,0:T(8,128)(2,1)S(1)} collective-permute-done((bf16[56,2048]{1,0:T(8,128)(2,1)S(1)}, bf16[56,2048]{1,0:T(8,128)(2,1)S(1)}, u32[]{:S(2)}, u32[]{:S(2)}) %collective-permute-start.36) | collective-permute-done | bytes 229408 | tf_op jit(solution)/shard_map/input_grad/ppermute | solution.py:156
  371.9 13.1 %all-to-all-done = bf16[4,56,1024]{2,1,0:T(8,128)(2,1)S(1)} async-done(((bf16[4,56,1024]{2,1,0:T(8,128)(2,1)}), bf16[4,56,1024]{2,1,0:T(8,128)(2,1)S(1)}, u32[]{:S(2)}, u32[]{:S(2)}) %all-to-all-start) | async-done | bytes 458784 | tf_op jit(solution)/shard_map/layer_out/all_to_all | solution.py:357
  (222 shorter events, 124.9 us)
Async XLA Ops:
  7.2 95.8 %all-gather.4.cloned.1.call-start = ((), (), s32[]{:S(2)}) async-start(), calls=%async_computation.2 | async-start | bytes 2293760 | tf_op jit(solution)/shard_map/token_rows/all_gather | solution.py:280
  10.9 171.8 %all-gather.6.cloned.1.call-start = ((), (), s32[]{:S(2)}) async-start(), calls=%async_computation.3 | async-start | bytes 9175040 | tf_op jit(solution)/shard_map/token_rows/all_gather | solution.py:283
  14.1 25.4 %collective-permute-start.3 = (bf16[64,1024]{1,0:T(8,128)(2,1)S(1)}, bf16[64,1024]{1,0:T(8,128)(2,1)S(1)}, u32[]{:S(2)}, u32[]{:S(2)}) collective-permute-start(bf16[64,1024]{1,0:T(8,128)(2,1)S(1)} %get-tuple-element.176), channel_id=1, source_target_pairs={{0,24},{8,16},{16,8},{24,0},{1,25},{9,17},{17,9},{25,1},{2,26},{10... | collective-permute-start | bytes 393224 | tf_op jit(solution)/shard_map/grad_rows/ppermute | solution.py:156
  16.6 22.9 %collective-permute-start.2 = (bf16[64,1024]{1,0:T(8,128)(2,1)S(1)}, bf16[64,1024]{1,0:T(8,128)(2,1)S(1)}, u32[]{:S(2)}, u32[]{:S(2)}) collective-permute-start(bf16[64,1024]{1,0:T(8,128)(2,1)S(1)} %get-tuple-element.178), channel_id=1, source_target_pairs={{0,16},{8,24},{16,0},{24,8},{1,17},{9,25},{17,1},{25,9},{2,18},{10... | collective-permute-start | bytes 393224 | tf_op jit(solution)/shard_map/grad_rows/ppermute | solution.py:156
  39.7 59.9 %collective-permute-start.11 = (bf16[1024,512]{1,0:T(8,128)(2,1)S(1)}, bf16[1024,512]{1,0:T(8,128)(2,1)S(1)}, u32[]{:S(2)}, u32[]{:S(2)}) collective-permute-start(bf16[1024,512]{1,0:T(8,128)(2,1)S(1)} %copy-done.37), channel_id=1, source_target_pairs={{0,8},{8,0},{16,24},{24,16},{1,9},{9,1},{17,25},{25,17},{2,10},{10... | collective-permute-start | bytes 3145736 | tf_op jit(solution)/shard_map/grad_rows/ppermute | solution.py:156
  42.5 60.5 %collective-permute-start.12 = (bf16[1024,512]{1,0:T(8,128)(2,1)S(1)}, bf16[1024,512]{1,0:T(8,128)(2,1)}, u32[]{:S(2)}, u32[]{:S(2)}) collective-permute-start(bf16[1024,512]{1,0:T(8,128)(2,1)S(1)} %copy-done.36), channel_id=1, source_target_pairs={{0,16},{8,24},{16,0},{24,8},{1,17},{9,25},{17,1},{25,9},{2,18},{10... | collective-permute-start | bytes 3145736 | tf_op jit(solution)/shard_map/grad_rows/ppermute | solution.py:156
  48.4 24.6 %collective-permute-start.8 = (bf16[224,1024]{1,0:T(8,128)(2,1)S(1)}, bf16[224,1024]{1,0:T(8,128)(2,1)S(1)}, u32[]{:S(2)}, u32[]{:S(2)}) collective-permute-start(bf16[224,1024]{1,0:T(8,128)(2,1)S(1)} %bitcast.103), channel_id=1, source_target_pairs={{0,5},{1,4},{2,7},{3,6},{4,1},{5,0},{6,3},{7,2},{8,13},{9,12},{10,... | collective-permute-start | bytes 1376264 | tf_op jit(solution)/shard_map/grad_rows/ppermute | solution.py:220
  53.2 29.6 %collective-permute-start.7 = (bf16[224,1024]{1,0:T(8,128)(2,1)S(1)}, bf16[224,1024]{1,0:T(8,128)(2,1)S(1)}, u32[]{:S(2)}, u32[]{:S(2)}) collective-permute-start(bf16[224,1024]{1,0:T(8,128)(2,1)S(1)} %bitcast.104), channel_id=1, source_target_pairs={{0,4},{1,5},{2,6},{3,7},{4,0},{5,1},{6,2},{7,3},{8,12},{9,13},{10,... | collective-permute-start | bytes 1376264 | tf_op jit(solution)/shard_map/grad_rows/ppermute | solution.py:220
  63.3 19.8 %collective-permute-start.6 = (bf16[224,1024]{1,0:T(8,128)(2,1)S(1)}, bf16[224,1024]{1,0:T(8,128)(2,1)S(1)}, u32[]{:S(2)}, u32[]{:S(2)}) collective-permute-start(bf16[224,1024]{1,0:T(8,128)(2,1)S(1)} %bitcast.105), channel_id=1, source_target_pairs={{0,3},{1,2},{2,1},{3,0},{4,7},{5,6},{6,5},{7,4},{8,11},{9,10},{10,... | collective-permute-start | bytes 1376264 | tf_op jit(solution)/shard_map/grad_rows/ppermute | solution.py:220
  103.0 201.2 %all-gather.8.cloned.1.call-start = ((), (), s32[]{:S(2)}) async-start(), calls=%async_computation.4 | async-start | bytes 4587520 | tf_op jit(solution)/shard_map/forward/all_gather | solution.py:311
  103.1 45.4 %collective-permute-start.15 = (bf16[1024,512]{1,0:T(8,128)(2,1)}, bf16[1024,512]{1,0:T(8,128)(2,1)S(1)}, u32[]{:S(2)}, u32[]{:S(2)}) collective-permute-start(bf16[1024,512]{1,0:T(8,128)(2,1)} %get-tuple-element.94), channel_id=1, source_target_pairs={{0,24},{8,16},{16,8},{24,0},{1,25},{9,17},{17,9},{25,1},{2,26},{10... | collective-permute-start | bytes 3145736 | tf_op jit(solution)/shard_map/hidden_grad/ppermute | solution.py:156
  113.4 35.0 %collective-permute-start.13 = (bf16[1792,256]{1,0:T(8,128)(2,1)S(1)}, bf16[1792,256]{1,0:T(8,128)(2,1)S(1)}, u32[]{:S(2)}, u32[]{:S(2)}) collective-permute-start(bf16[1792,256]{1,0:T(8,128)(2,1)S(1)} %get-tuple-element.142), channel_id=1, source_target_pairs={{0,8},{1,9},{2,10},{3,11},{4,12},{5,13},{6,14},{7,15}} | collective-permute-start | bytes 2752520 | tf_op jit(solution)/shard_map/hidden_grad/ppermute | solution.py:172
  157.9 35.4 %collective-permute-start.17 = (bf16[1792,256]{1,0:T(8,128)(2,1)}, bf16[1792,256]{1,0:T(8,128)(2,1)S(1)}, u32[]{:S(2)}, u32[]{:S(2)}) collective-permute-start(bf16[1792,256]{1,0:T(8,128)(2,1)} %get-tuple-element.139), channel_id=1, source_target_pairs={{16,8},{24,16},{17,9},{25,17},{18,10},{26,18},{19,11},{27,19},{20,... | collective-permute-start | bytes 2752520 | tf_op jit(solution)/shard_map/forward/ppermute | solution.py:173
  158.7 34.7 %collective-permute-start.16 = (bf16[1792,256]{1,0:T(8,128)(2,1)}, bf16[1792,256]{1,0:T(8,128)(2,1)}, u32[]{:S(2)}, u32[]{:S(2)}) collective-permute-start(bf16[1792,256]{1,0:T(8,128)(2,1)} %get-tuple-element.140), channel_id=1, source_target_pairs={{0,8},{8,16},{1,9},{9,17},{2,10},{10,18},{3,11},{11,19},{4,12},{12... | collective-permute-start | bytes 2752520 | tf_op jit(solution)/shard_map/forward/ppermute | solution.py:172
  203.2 24.9 %collective-permute-start.20 = (bf16[1792,256]{1,0:T(8,128)(2,1)}, bf16[1792,256]{1,0:T(8,128)(2,1)S(1)}, u32[]{:S(2)}, u32[]{:S(2)}) collective-permute-start(bf16[1792,256]{1,0:T(8,128)(2,1)} %get-tuple-element.137), channel_id=1, source_target_pairs={{8,0},{16,8},{24,16},{9,1},{17,9},{25,17},{10,2},{18,10},{26,18},{... | collective-permute-start | bytes 2752520 | tf_op jit(solution)/shard_map/forward/ppermute | solution.py:173
  204.5 24.9 %collective-permute-start.19 = (bf16[1792,256]{1,0:T(8,128)(2,1)}, bf16[1792,256]{1,0:T(8,128)(2,1)}, u32[]{:S(2)}, u32[]{:S(2)}) collective-permute-start(bf16[1792,256]{1,0:T(8,128)(2,1)} %get-tuple-element.138), channel_id=1, source_target_pairs={{0,8},{8,16},{16,24},{1,9},{9,17},{17,25},{2,10},{10,18},{18,26},{... | collective-permute-start | bytes 2752520 | tf_op jit(solution)/shard_map/forward/ppermute | solution.py:172
  231.0 135.1 %reduce-scatter.2.cloned.1.call-start = ((), (), s32[]{:S(2)}) async-start(), calls=%async_computation.5 | async-start | bytes 4128768 | tf_op jit(solution)/shard_map/input_grad/reduce_scatter | solution.py:347
  237.9 21.8 %collective-permute-start.25 = (bf16[448,1024]{1,0:T(8,128)(2,1)S(1)}, bf16[448,1024]{1,0:T(8,128)(2,1)S(1)}, u32[]{:S(2)}, u32[]{:S(2)}) collective-permute-start(bf16[448,1024]{1,0:T(8,128)(2,1)S(1)} %convolution_convert_fusion.3), channel_id=1, source_target_pairs={{0,4},{1,5},{2,6},{3,7},{4,0},{5,1},{6,2},{7,3},{8,12},{9,13},{10,... | collective-permute-start | bytes 2752520 | tf_op jit(solution)/shard_map/input_grad/ppermute | solution.py:236
  240.8 21.9 %collective-permute-start.23 = (bf16[448,1024]{1,0:T(8,128)(2,1)S(1)}, bf16[448,1024]{1,0:T(8,128)(2,1)S(1)}, u32[]{:S(2)}, u32[]{:S(2)}) collective-permute-start(bf16[448,1024]{1,0:T(8,128)(2,1)S(1)} %convolution_convert_fusion.4), channel_id=1, source_target_pairs={{0,2},{1,3},{2,0},{3,1},{4,6},{5,7},{6,4},{7,5},{8,10},{9,11},{10,... | collective-permute-start | bytes 2752520 | tf_op jit(solution)/shard_map/input_grad/ppermute | solution.py:236
  241.8 22.0 %collective-permute-start.27 = (bf16[896,512]{1,0:T(8,128)(2,1)S(1)}, bf16[896,512]{1,0:T(8,128)(2,1)S(1)}, u32[]{:S(2)}, u32[]{:S(2)}) collective-permute-start(bf16[896,512]{1,0:T(8,128)(2,1)S(1)} %fusion.5), channel_id=1, source_target_pairs={{0,1},{1,0},{2,3},{3,2},{4,5},{5,4},{6,7},{7,6},{8,9},{9,8},{10,11... | collective-permute-start | bytes 2752520 | tf_op jit(solution)/shard_map/input_grad/ppermute | solution.py:327
  318.5 24.4 %collective-permute-start.34 = (bf16[224,1024]{1,0:T(8,128)(2,1)S(1)}, bf16[224,1024]{1,0:T(8,128)(2,1)S(1)}, u32[]{:S(2)}, u32[]{:S(2)}) collective-permute-start(bf16[224,1024]{1,0:T(8,128)(2,1)S(1)} %fusion.13), channel_id=1, source_target_pairs={{0,2},{1,3},{2,0},{3,1},{4,6},{5,7},{6,4},{7,5},{8,10},{9,11},{10,... | collective-permute-start | bytes 1376264 | tf_op jit(solution)/shard_map/input_grad/ppermute | solution.py:236
  321.1 22.6 %collective-permute-start.33 = (bf16[224,1024]{1,0:T(8,128)(2,1)S(1)}, bf16[224,1024]{1,0:T(8,128)(2,1)S(1)}, u32[]{:S(2)}, u32[]{:S(2)}) collective-permute-start(bf16[224,1024]{1,0:T(8,128)(2,1)S(1)} %fusion.12), channel_id=1, source_target_pairs={{0,4},{1,5},{2,6},{3,7},{4,0},{5,1},{6,2},{7,3},{8,12},{9,13},{10,... | collective-permute-start | bytes 1376264 | tf_op jit(solution)/shard_map/input_grad/ppermute | solution.py:236
  323.0 19.9 %collective-permute-start.29 = (bf16[56,2048]{1,0:T(8,128)(2,1)S(1)}, bf16[56,2048]{1,0:T(8,128)(2,1)S(1)}, u32[]{:S(2)}, u32[]{:S(2)}) collective-permute-start(bf16[56,2048]{1,0:T(8,128)(2,1)S(1)} %get-tuple-element.159), channel_id=1, source_target_pairs={{0,16},{8,24},{16,0},{24,8},{1,17},{9,25},{17,1},{25,9},{2,18},{10... | collective-permute-start | bytes 688136 | tf_op jit(solution)/shard_map/input_grad/ppermute | solution.py:156
  323.2 19.8 %collective-permute-start.28 = (bf16[56,2048]{1,0:T(8,128)(2,1)S(1)}, bf16[56,2048]{1,0:T(8,128)(2,1)S(1)}, u32[]{:S(2)}, u32[]{:S(2)}) collective-permute-start(bf16[56,2048]{1,0:T(8,128)(2,1)S(1)} %get-tuple-element.160), channel_id=1, source_target_pairs={{0,8},{8,0},{16,24},{24,16},{1,9},{9,1},{17,25},{25,17},{2,10},{10... | collective-permute-start | bytes 688136 | tf_op jit(solution)/shard_map/input_grad/ppermute | solution.py:156
  (59 other events, 606.5 us)
Sparse Core Ops, SparseCore 0:
  11.0 70.5 all-gather.3
  103.2 79.4 all-gather.5
  231.1 73.0 all-gather.7
  312.9 46.9 reduce-scatter.1
